TPU v7x, 256 devices: a whole 4x4x8 slice. The times are simulated.
256 devices in a mesh: dp: 256 (over z, y, x, core).
Axes of the slice: x: 4, y: 4, z: 8, core: 2. Of those that a mesh axis runs over, the one named last changes fastest.
Arguments:
- image_emb: bfloat16 [262144, 1152], P('dp'), may hold values from -0.1875 to 0.1875
- text_emb: bfloat16 [262144, 1152], P('dp'), may hold values from -0.1875 to 0.1875
- cosine_multiplier: float32 [1], replicated, may hold values from 5 to 20
- logit_bias: float32 [1], replicated, may hold values from -5 to -2
Outputs:
- image_grad: bfloat16 [262144, 1152], P('dp')
- text_grad: bfloat16 [262144, 1152], P('dp')
All inputs are finite; a program needn't handle non-finite values.
Results may differ from a plain program's by a relative error of at most 0.0063.
Values may be sent and summed in bfloat16 or wider, within the bound.
No kernel may reach another device: no remote copies, remote signals or barrier semaphores. Data moves between devices by JAX's collectives and lax.ppermute only.
A program may use at most 64 MiB of HBM per device.

v0:
```python
import jax
import jax.numpy as jnp
from jax import lax
from jax.sharding import PartitionSpec as P

epsilon = 1e-06


def from_behind(value, axis, steps):
    count = lax.axis_size(axis)
    pairs = [(source, (source + steps) % count) for source in range(count)]
    return lax.ppermute(value, axis, pairs)


def normalize(values):
    floats = values.astype(jnp.float32)
    inverse = lax.rsqrt(jnp.sum(floats * floats, axis=-1, keepdims=True) + epsilon)
    return (floats * inverse, inverse)


def norm_backward(normed, inverse, upstream):
    inner = jnp.sum(normed * upstream, axis=-1, keepdims=True)
    return (inverse * (upstream - normed * inner)).astype(jnp.bfloat16)


def objective_factors(
    picture_count, caption_count, steepness_factor, moved_intercept, matching_indicator
):
    unscaled_agreement = lax.dot_general(
        picture_count, caption_count, (((1,), (1,)), ((), ())), preferred_element_type=jnp.float32
    )
    couple_scores = steepness_factor * unscaled_agreement + moved_intercept
    if matching_indicator:
        desired_signs = 2.0 * jnp.eye(picture_count.shape[0], dtype=jnp.float32) - 1.0
        couple_factors = (
            -desired_signs * jax.nn.sigmoid(-desired_signs * couple_scores) * steepness_factor
        )
    else:
        couple_factors = jax.nn.sigmoid(couple_scores) * steepness_factor
    return couple_factors.astype(jnp.bfloat16)


def left_product(couple_factors, picture_count):
    return lax.dot_general(
        couple_factors, picture_count, (((0,), (0,)), ((), ())), preferred_element_type=jnp.float32
    )


def on_device(image_emb, text_emb, cosine_multiplier, logit_bias):
    steepness_factor = cosine_multiplier[0]
    moved_intercept = logit_bias[0]
    y_img, inv_img = normalize(image_emb)
    y_txt, inv_txt = normalize(text_emb)
    picture_features = y_img.astype(jnp.bfloat16)
    caption_features = y_txt.astype(jnp.bfloat16)
    resident_weights = objective_factors(
        picture_features, caption_features, steepness_factor, moved_intercept, True
    )
    image_total = jnp.dot(resident_weights, caption_features, preferred_element_type=jnp.float32)
    text_total = left_product(resident_weights, picture_features)
    neighbour_processor = from_behind(caption_features, "dp", 1)
    couple_factors = objective_factors(
        picture_features, neighbour_processor, steepness_factor, moved_intercept, False
    )
    image_total = image_total + jnp.dot(
        couple_factors, neighbour_processor, preferred_element_type=jnp.float32
    )
    partial_grad = left_product(couple_factors, picture_features).astype(jnp.bfloat16)
    returned = from_behind(partial_grad, "dp", -1)
    text_total = text_total + returned.astype(jnp.float32)
    return (norm_backward(y_img, inv_img, image_total), norm_backward(y_txt, inv_txt, text_total))


def solution(mesh):
    in_specs = (P("dp", None), P("dp", None), P(), P())
    out_specs = (P("dp", None), P("dp", None))
    return jax.shard_map(
        on_device, mesh=mesh, in_specs=in_specs, out_specs=out_specs, check_vma=False
    )
```

profile of v0, /device:TPU:127, one launch (start us, length us, event | category | flops | bytes accessed | tf_op | source)
XLA Modules:
  0.0 82.3 jit_solution(9102095732491626992)
XLA Ops:
  0.6 0.0 copy-start.1
  0.6 2.3 %fusion.15 = f32[1024]{0:T(1024)S(1)} fusion(bf16[1024,1152]{1,0:T(8,128)(2,1)} %param.5), kind=kLoop, calls=%fused_computation.19 | loop fusion | flops 3537920 | bytes 2363392 | tf_op jit(solution)/shard_map/reduce_sum | solution.py:17
  3.0 2.1 %fusion.2 = bf16[1024,1152]{1,0:T(8,128)(2,1)S(1)} fusion(bf16[1024,1152]{1,0:T(8,128)(2,1)} %param.5, f32[1024]{0:T(1024)S(1)} %add_rsqrt_fusion), kind=kLoop, calls=%fused_computation.4 | loop fusion | flops 3538944 | bytes 4722688 | tf_op jit(solution)/shard_map/convert_element_type | solution.py:55
  5.1 3.1 %collective-permute-start = (bf16[1024,1152]{1,0:T(8,128)(2,1)S(1)}, bf16[1024,1152]{1,0:T(8,128)(2,1)S(1)}, u32[]{:S(2)}, u32[]{:S(2)}) collective-permute-start(bf16[1024,1152]{1,0:T(8,128)(2,1)S(1)} %fusion.2), channel_id=1, source_target_pairs={{0,1},{1,2},{2,3},{3,4},{4,5},{5,6},{6,7},{7,8},{8,9},{9,10},{10,1... | collective-permute-start | bytes 7077896 | tf_op jit(solution)/shard_map/ppermute | solution.py:12
  9.5 0.0 copy-done.1
  9.5 0.5 fusion.10
  10.0 23.9 %collective-permute-done = bf16[1024,1152]{1,0:T(8,128)(2,1)S(1)} collective-permute-done((bf16[1024,1152]{1,0:T(8,128)(2,1)S(1)}, bf16[1024,1152]{1,0:T(8,128)(2,1)S(1)}, u32[]{:S(2)}, u32[]{:S(2)}) %collective-permute-start) | collective-permute-done | bytes 2359328 | tf_op jit(solution)/shard_map/ppermute | solution.py:12
  34.0 3.8 %multiply_convert_fusion = bf16[1024,1024]{1,0:T(8,128)(2,1)S(1)} fusion(bf16[1024,1152]{1,0:T(8,128)(2,1)S(1)} %collective-permute-done, f32[]{:T(128)} %bitcast.13, f32[]{:T(128)} %bitcast.10, bf16[1024,1152]{1,0:T(8,128)(2,1)S(1)} %copy-done.1, f32[1024]{0:T(1024)S(1)} %add_rsqrt_fusion.1), kind=kOutput, calls=%fused_computation.22 | convolution fusion | flops 2426798080 | bytes 6819848 | tf_op jit(solution)/shard_map/dot_general | solution.py:29
  37.7 3.5 %convolution_convert_fusion = bf16[1024,1152]{1,0:T(8,128)(2,1)S(1)} fusion(bf16[1024,1024]{1,0:T(8,128)(2,1)S(1)} %multiply_convert_fusion, bf16[1024,1152]{1,0:T(8,128)(2,1)S(1)} %copy-done.1, f32[1024]{0:T(1024)S(1)} %add_rsqrt_fusion.1), kind=kOutput, calls=%fused_computation.25 | convolution fusion | flops 2420637696 | bytes 6819840 | tf_op jit(solution)/shard_map/dot_general | solution.py:44
  41.2 0.4 collective-permute-start.1
  41.7 4.7 %multiply_convert_fusion.1 = bf16[1024,1024]{1,0:T(8,128)(2,1)S(1)} fusion(bf16[1024,1152]{1,0:T(8,128)(2,1)S(1)} %fusion.2, f32[]{:T(128)} %bitcast.12, f32[]{:T(128)} %bitcast.11, bf16[1024,1152]{1,0:T(8,128)(2,1)S(1)} %copy-done.1, f32[1024]{0:T(1024)S(1)} %add_rsqrt_fusion.1), kind=kOutput, calls=%fused_computation.23 | convolution fusion | flops 2433089536 | bytes 6819848 | tf_op jit(solution)/shard_map/dot_general | solution.py:29
  46.3 2.9 %fusion.21 = f32[1024,1152]{1,0:T(8,128)S(1)} fusion(bf16[1024,1024]{1,0:T(8,128)(2,1)S(1)} %multiply_convert_fusion.1, bf16[1024,1152]{1,0:T(8,128)(2,1)S(1)} %fusion.2), kind=kOutput, calls=%fused_computation.29 | convolution fusion | flops 2415919104 | bytes 9175040 | tf_op jit(solution)/shard_map/dot_general | solution.py:59
  49.2 3.2 %fusion.6 = (f32[1024]{0:T(1024)S(1)}, f32[1024,1152]{1,0:T(8,128)S(1)}) fusion(bf16[1024,1152]{1,0:T(8,128)(2,1)S(1)} %copy-done.1, f32[1024]{0:T(1024)S(1)} %add_rsqrt_fusion.1, f32[1024,1152]{1,0:T(8,128)S(1)} %fusion.21, bf16[1024,1024]{1,0:T(8,128)(2,1)S(1)} %multiply_convert_fusion, bf16[1024,1152]{1,0:T(8,128)(2,1)S(1)} %collective-permute-done), kind=kOutput, calls=%fused_computation.10 | convolution fusion | flops 2421816320 | bytes 16261120 | tf_op jit(solution)/shard_map/dot_general | solution.py:65
  52.5 0.0 copy-start
  52.5 2.3 %fusion.9 = bf16[1024,1152]{1,0:T(8,128)(2,1)} fusion(f32[1024,1152]{1,0:T(8,128)S(1)} %get-tuple-element.3, bf16[1024,1152]{1,0:T(8,128)(2,1)S(1)} %copy-done.1, f32[1024]{0:T(1024)S(1)} %get-tuple-element.2, f32[1024]{0:T(1024)S(1)} %add_rsqrt_fusion.1), kind=kLoop, calls=%fused_computation.13 | loop fusion | flops 7077888 | bytes 9445376 | tf_op jit(solution)/shard_map/convert_element_type | solution.py:23
  54.8 21.1 %collective-permute-done.1 = bf16[1024,1152]{1,0:T(8,128)(2,1)S(1)} collective-permute-done((bf16[1024,1152]{1,0:T(8,128)(2,1)S(1)}, bf16[1024,1152]{1,0:T(8,128)(2,1)S(1)}, u32[]{:S(2)}, u32[]{:S(2)}) %collective-permute-start.1) | collective-permute-done | bytes 2359328 | tf_op jit(solution)/shard_map/ppermute | solution.py:12
  75.9 0.0 copy-done
  75.9 3.8 %fusion.11 = (f32[1024]{0:T(1024)S(1)}, f32[1024,1152]{1,0:T(8,128)S(1)}) fusion(bf16[1024,1152]{1,0:T(8,128)(2,1)S(1)} %copy-done, bf16[1024,1152]{1,0:T(8,128)(2,1)S(1)} %collective-permute-done.1, f32[1024]{0:T(1024)S(1)} %add_rsqrt_fusion, bf16[1024,1024]{1,0:T(8,128)(2,1)S(1)} %multiply_convert_fusion.1, bf16[1024,1152]{1,0:T(8,128)(2,1)S(1)} %copy-done.1, ...), kind=kOutput, calls=%fused_computation.15 | convolution fusion | flops 2426534912 | bytes 13905920 | tf_op jit(solution)/shard_map/dot_general | solution.py:44
  79.8 2.6 %fusion.14 = bf16[1024,1152]{1,0:T(8,128)(2,1)} fusion(bf16[1024,1152]{1,0:T(8,128)(2,1)S(1)} %copy-done, f32[1024,1152]{1,0:T(8,128)S(1)} %get-tuple-element.5, bf16[1024,1152]{1,0:T(8,128)(2,1)S(1)} %collective-permute-done.1, f32[1024]{0:T(1024)S(1)} %get-tuple-element.4, f32[1024]{0:T(1024)S(1)} %add_rsqrt_fusion), kind=kLoop, calls=%fused_computation.18 | loop fusion | flops 9437184 | bytes 11804672 | tf_op jit(solution)/shard_map/convert_element_type | solution.py:23
  (2 shorter events, 0.0 us)
Async XLA Ops:
  0.6 8.9 %copy-start.1 = (bf16[1024,1152]{1,0:T(8,128)(2,1)S(1)}, bf16[1024,1152]{1,0:T(8,128)(2,1)}, u32[]{:S(2)}) copy-start(bf16[1024,1152]{1,0:T(8,128)(2,1)} %param.4) | copy-start | bytes 7077892
  5.1 28.8 %collective-permute-start = (bf16[1024,1152]{1,0:T(8,128)(2,1)S(1)}, bf16[1024,1152]{1,0:T(8,128)(2,1)S(1)}, u32[]{:S(2)}, u32[]{:S(2)}) collective-permute-start(bf16[1024,1152]{1,0:T(8,128)(2,1)S(1)} %fusion.2), channel_id=1, source_target_pairs={{0,1},{1,2},{2,3},{3,4},{4,5},{5,6},{6,7},{7,8},{8,9},{9,10},{10,1... | collective-permute-start | bytes 7077896 | tf_op jit(solution)/shard_map/ppermute | solution.py:12
  41.2 34.7 %collective-permute-start.1 = (bf16[1024,1152]{1,0:T(8,128)(2,1)S(1)}, bf16[1024,1152]{1,0:T(8,128)(2,1)S(1)}, u32[]{:S(2)}, u32[]{:S(2)}) collective-permute-start(bf16[1024,1152]{1,0:T(8,128)(2,1)S(1)} %convolution_convert_fusion), channel_id=1, source_target_pairs={{0,255},{1,0},{2,1},{3,2},{4,3},{5,4},{6,5},{7,6},{8,7},{9,8},{10,... | collective-permute-start | bytes 7077896 | tf_op jit(solution)/shard_map/ppermute | solution.py:12
  52.5 23.5 %copy-start = (bf16[1024,1152]{1,0:T(8,128)(2,1)S(1)}, bf16[1024,1152]{1,0:T(8,128)(2,1)}, u32[]{:S(2)}) copy-start(bf16[1024,1152]{1,0:T(8,128)(2,1)} %param.5) | copy-start | bytes 7077892
where the time goes:
time: 82.5 us; the launch traced here: 82.3 us
  waiting for transfers between devices  45.1 us (55%)
  matrix products  21.9 us (27%)
  other arithmetic  9.88 us (12%)
  starting transfers between devices  3.49 us (4%)
  between operations  2.01 us (2%)
    ppermute x2, waiting for transfers between devices, from_behind(): return lax.ppermute(value, axis, pairs)  45.1 us
    dot_general x2, matrix products, objective_factors(): lax.dot_general(picture_count, caption_count, (((1,), (1,)), ((), ())), p...  8.43 us
    dot_general x2, matrix products, left_product(): lax.dot_general(couple_factors, picture_count, (((0,), (0,)), ((), ())),...  7.33 us
    convert_element_type x2, other arithmetic, norm_backward(): return (inverse * (upstream - normed * inner)).astype(jnp.bfloat16)  4.88 us
    ppermute x2, starting transfers between devices, from_behind(): return lax.ppermute(value, axis, pairs)  3.49 us
    dot_general x1, matrix products, on_device(): jnp.dot(couple_factors, neighbour_processor, preferred_element_type=jnp.f...  3.23 us
    dot_general x1, matrix products, on_device(): jnp.dot(resident_weights, caption_features, preferred_element_type=jnp.fl...  2.88 us
    reduce_sum x2, other arithmetic, normalize(): jnp.sum(floats * floats, axis=-1, keepdims=True) + epsilon  2.87 us
  transfers between devices with their start and end apart: 2, of which 2 were waited for; matrix products, arithmetic and copies ran while one was open for 17% of the time, Pallas kernels for 0%

commit v1 on v0

v1 whole, which is shorter than its diff:
```python
import functools

import jax
import jax.numpy as jnp
from jax import lax
from jax.experimental import pallas as pl
from jax.experimental.pallas import tpu as pltpu
from jax.sharding import PartitionSpec as P

epsilon = 1e-06
LOG2_E = 1.4426950408889634
F32, BF16 = jnp.float32, jnp.bfloat16
BLOCK = 256
FIRST = 768
MIB = 2**20

VMEM = pl.BlockSpec(memory_space=pltpu.VMEM)
SMEM = pl.BlockSpec(memory_space=pltpu.SMEM)
HBM = pl.BlockSpec(memory_space=pl.ANY)


def rows_dot_rows(a, b):
    return lax.dot_general(a, b, (((1,), (1,)), ((), ())), preferred_element_type=F32)


def columns_dot(a, b):
    return lax.dot_general(a, b, (((0,), (0,)), ((), ())), preferred_element_type=F32)


def dot(a, b):
    return jnp.dot(a, b, preferred_element_type=F32)


def blocks(rows):
    return [slice(start, start + BLOCK) for start in range(0, rows, BLOCK)]


def fetch(parity, if_even, if_odd, start, target, sems):
    for i, here in enumerate(blocks(target.shape[0])):
        there = pl.ds(start + here.start, BLOCK)

        @pl.when(parity == 0)
        def _():
            pltpu.make_async_copy(if_even.at[there], target.at[here], sems.at[i]).start()

        @pl.when(parity == 1)
        def _():
            pltpu.make_async_copy(if_odd.at[there], target.at[here], sems.at[i]).start()


def arrived(source, target, sems, i, here):
    pltpu.make_async_copy(source.at[pl.ds(0, BLOCK)], target.at[here], sems.at[i]).wait()


def normalize_block(raw):
    floats = raw.astype(F32)
    inverse = lax.rsqrt(jnp.sum(floats * floats, axis=-1, keepdims=True) + epsilon)
    return (floats * inverse).astype(BF16), inverse


def first_kernel(parity_ref, image, text, z1, raw1, inv1, sems):
    fetch(parity_ref[0], image, text, 0, raw1, sems)
    for i, here in enumerate(blocks(raw1.shape[0])):
        arrived(image, raw1, sems, i, here)
        z1[here, :], inv1[here, :] = normalize_block(raw1[here, :])


def rest_kernel(
    parity_ref, image, text, z1, zp, z2, zq, rawp, raw2, invp, inv2, semsp, sems2
):
    first = z1.shape[0]
    fetch(parity_ref[0], text, image, 0, rawp, semsp)
    fetch(parity_ref[0], image, text, first, raw2, sems2)
    for i, here in enumerate(blocks(rawp.shape[0])):
        arrived(image, rawp, semsp, i, here)
        zp[here, :], invp[here, :] = normalize_block(rawp[here, :])
    zq[:first, :] = z1[...]
    for i, here in enumerate(blocks(raw2.shape[0])):
        arrived(image, raw2, sems2, i, here)
        normed, inv2[here, :] = normalize_block(raw2[here, :])
        z2[here, :] = normed
        zq[pl.ds(first + here.start, BLOCK), :] = normed


def exponential(agreement, scale, shift):
    return jnp.exp2(agreement * scale + shift)


def local_kernel(multiplier_ref, bias_ref, zp, zq, coef, gq):
    multiplier = multiplier_ref[0]
    scale, shift = -multiplier * LOG2_E, -bias_ref[0] * LOG2_E
    count = zq.shape[0]
    for here in blocks(zp.shape[0]):
        power = exponential(rows_dot_rows(zp[here, :], zq[...]), scale, shift)
        value = multiplier / (1.0 + power)
        row = lax.broadcasted_iota(jnp.int32, (BLOCK, count), 0) + here.start
        column = lax.broadcasted_iota(jnp.int32, (BLOCK, count), 1)
        coef[here, :] = jnp.where(row == column, -power * value, value).astype(BF16)
    for here in blocks(count):
        gq[here, :] = columns_dot(coef[:, here], zp[...])


def remote_coef(own, other, multiplier, scale, shift):
    power = exponential(rows_dot_rows(own, other), scale, shift)
    return (multiplier / (1.0 + power)).astype(BF16)


def backward_block(raw, inverse, upstream):
    floats = raw.astype(F32)
    inner = jnp.sum(floats * upstream, axis=-1, keepdims=True)
    return (inverse * (upstream - floats * (inverse * inverse * inner))).astype(BF16)


def put(parity, if_even, if_odd, there, source, sem):
    @pl.when(parity == 0)
    def _():
        pltpu.make_async_copy(source, if_even.at[there], sem).start()

    @pl.when(parity == 1)
    def _():
        pltpu.make_async_copy(source, if_odd.at[there], sem).start()


def near_kernel(
    parity_ref, multiplier_ref, bias_ref, zp, zq, coef, other, rawp, invp, image_out, text_out, token, held, sems
):
    token[...] = jnp.zeros_like(token)
    multiplier = multiplier_ref[0]
    scale, shift = -multiplier * LOG2_E, -bias_ref[0] * LOG2_E
    for i, here in enumerate(blocks(zp.shape[0])):
        factors = remote_coef(zp[here, :], other[...], multiplier, scale, shift)
        total = dot(coef[here, :], zq[...]) + dot(factors, other[...])
        held[here, :] = backward_block(rawp[here, :], invp[here, :], total)
        put(parity_ref[0], text_out, image_out, here, held.at[here], sems.at[i])
    for i, here in enumerate(blocks(zp.shape[0])):
        pltpu.make_async_copy(held.at[here], image_out.at[here], sems.at[i]).wait()


def far_kernel(multiplier_ref, bias_ref, zq, other, gq, after_near, total):
    multiplier = multiplier_ref[0]
    scale, shift = -multiplier * LOG2_E, -bias_ref[0] * LOG2_E
    for here in blocks(zq.shape[0]):
        factors = remote_coef(zq[here, :], other[...], multiplier, scale, shift)
        total[here, :] = gq[here, :] + dot(factors, other[...])


def last_kernel(
    parity_ref, multiplier_ref, bias_ref, zq, other, gq, raw1, raw2, inv1, inv2, image_in, text_in, image_out, text_out, held, sems
):
    multiplier = multiplier_ref[0]
    scale, shift = -multiplier * LOG2_E, -bias_ref[0] * LOG2_E
    first = raw1.shape[0]
    for i, here in enumerate(blocks(zq.shape[0])):
        factors = remote_coef(zq[here, :], other[...], multiplier, scale, shift)
        total = gq[here, :] + dot(factors, other[...])
        if here.start < first:
            raw, inverse = raw1[here, :], inv1[here, :]
        else:
            there = slice(here.start - first, here.stop - first)
            raw, inverse = raw2[there, :], inv2[there, :]
        held[here, :] = backward_block(raw, inverse, total)
        put(parity_ref[0], image_out, text_out, here, held.at[here], sems.at[i])
    for i, here in enumerate(blocks(zq.shape[0])):
        pltpu.make_async_copy(held.at[here], image_out.at[here], sems.at[i]).wait()


def shape(rows, columns, kind):
    return jax.ShapeDtypeStruct((rows, columns), kind)


def call(kernel, out_shape, in_specs, out_specs, scratch, limit, flops, **more):
    return pl.pallas_call(
        kernel,
        out_shape=out_shape,
        in_specs=in_specs,
        out_specs=out_specs,
        scratch_shapes=scratch,
        compiler_params=pltpu.CompilerParams(vmem_limit_bytes=limit * MIB),
        cost_estimate=pl.CostEstimate(flops=flops // 64, bytes_accessed=1024, transcendentals=0),
        **more,
    )


def on_device(image_emb, text_emb, cosine_multiplier, logit_bias):
    rows, width = image_emb.shape
    count = lax.axis_size("dp")
    parity = (lax.axis_index("dp") % 2).astype(jnp.int32).reshape(1)
    near = [(e, e ^ 1) for e in range(count)]
    far = [(e, (e - 1) % count if e % 2 == 0 else (e + 1) % count) for e in range(count)]
    first, rest = FIRST, rows - FIRST
    image_emb = pltpu.with_memory_space_constraint(image_emb, pltpu.HBM)
    text_emb = pltpu.with_memory_space_constraint(text_emb, pltpu.HBM)
    dma = pltpu.SemaphoreType.DMA
    product = 2 * rows * rows * width

    z1, raw1, inv1 = call(
        first_kernel,
        (shape(first, width, BF16), shape(first, width, BF16), shape(first, 1, F32)),
        [SMEM, HBM, HBM], (VMEM,) * 3, [dma((first // BLOCK,))], 4, product // 8,
    )(parity, image_emb, text_emb)
    far1 = lax.ppermute(z1, "dp", far)
    zp, z2, zq, rawp, raw2, invp, inv2 = call(
        rest_kernel,
        (
            shape(rows, width, BF16), shape(rest, width, BF16), shape(rows, width, BF16),
            shape(rows, width, BF16), shape(rest, width, BF16), shape(rows, 1, F32), shape(rest, 1, F32),
        ),
        [SMEM, HBM, HBM, VMEM], (VMEM,) * 7, [dma((rows // BLOCK,)), dma((rest // BLOCK,))], 4, product // 4,
    )(parity, image_emb, text_emb, z1)
    near_block = lax.ppermute(zp, "dp", near)
    far2 = lax.ppermute(z2, "dp", far)
    coef, gq = call(
        local_kernel,
        (shape(rows, rows, BF16), shape(rows, width, F32)),
        [SMEM, SMEM, VMEM, VMEM], (VMEM,) * 2, [], 8, 2 * product,
    )(cosine_multiplier, logit_bias, zp, zq)
    image_out, text_out, token = call(
        near_kernel,
        (pltpu.HBM((rows, width), BF16),) * 2 + (shape(8, 128, F32),),
        [SMEM] * 3 + [VMEM] * 6, (HBM, HBM, VMEM),
        [pltpu.VMEM((rows, width), BF16), dma((rows // BLOCK,))], 12, 3 * product,
    )(parity, cosine_multiplier, logit_bias, zp, zq, coef, near_block, rawp, invp)
    gq = call(
        far_kernel, shape(rows, width, F32),
        [SMEM, SMEM, VMEM, VMEM, VMEM, VMEM], VMEM, [], 8, 2 * product * first // rows,
    )(cosine_multiplier, logit_bias, zq, far1, gq, token)
    return call(
        last_kernel,
        (pltpu.HBM((rows, width), BF16),) * 2,
        [SMEM] * 3 + [VMEM] * 7 + [HBM, HBM], (HBM, HBM),
        [pltpu.VMEM((rows, width), BF16), dma((rows // BLOCK,))], 12, 2 * product * rest // rows,
        input_output_aliases={10: 0, 11: 1},
    )(parity, cosine_multiplier, logit_bias, zq, far2, gq, raw1, raw2, inv1, inv2, image_out, text_out)


def solution(mesh):
    in_specs = (P("dp", None), P("dp", None), P(), P())
    out_specs = (P("dp", None), P("dp", None))
    return jax.shard_map(
        on_device, mesh=mesh, in_specs=in_specs, out_specs=out_specs, check_vma=False
    )
```

time: 82.5 us -> 44.7 us (0.54)
  the two profiles are of different devices: /device:TPU:127 before, /device:TPU:0 now
where the time goes in v1:
time: 44.7 us; the launch traced here: 44.5 us
  Pallas kernels  28.9 us (65%)
  starting transfers between devices  8.99 us (20%)
  waiting for transfers between devices  4.49 us (10%)
  between operations  2.17 us (5%)
    pallas_call x1, Pallas kernels, on_device(): call(near_kernel, (pltpu.HBM((rows, width), BF16),) * 2 + (shape(8, 128,...  10.1 us
    ppermute x1, starting transfers between devices, on_device(): far1 = lax.ppermute(z1, 'dp', far)  8.87 us
    pallas_call x1, Pallas kernels, on_device(): call(local_kernel, (shape(rows, rows, BF16), shape(rows, width, F32)), [S...  5.82 us
    pallas_call x1, Pallas kernels, on_device(): call(far_kernel, shape(rows, width, F32), [SMEM, SMEM, VMEM, VMEM, VMEM,...  4.75 us
    pallas_call x1, Pallas kernels, on_device(): call(last_kernel, (pltpu.HBM((rows, width), BF16),) * 2, [SMEM] * 3 + [VM...  4.21 us
    ppermute x1, waiting for transfers between devices, on_device(): far1 = lax.ppermute(z1, 'dp', far)  2.92 us
    pallas_call x1, Pallas kernels, on_device(): call(rest_kernel, (shape(rows, width, BF16), shape(rest, width, BF16), sh...  2.26 us
    pallas_call x1, Pallas kernels, on_device(): call(first_kernel, (shape(first, width, BF16), shape(first, width, BF16),...  1.7 us
  transfers between devices with their start and end apart: 3, of which 2 were waited for; matrix products, arithmetic and copies ran while one was open for 0% of the time, Pallas kernels for 46%

profile of v1, /device:TPU:0, one launch (start us, length us, event | category | flops | bytes accessed | tf_op | source)
XLA Modules:
  0.0 44.5 jit_solution(10449561602553142496)
XLA Ops:
  0.6 1.7 %shard_map.59 = (bf16[768,1152]{1,0:T(8,128)(2,1)S(1)}, bf16[768,1152]{1,0:T(8,128)(2,1)S(1)}, f32[768,1]{1,0:T(8,128)S(1)}) custom-call(s32[1]{0:T(128)} %bitcast.parity_ref, bf16[1024,1152]{1,0:T(8,128)(2,1)} %image.3, bf16[1024,1152]{1,0:T(8,128)(2,1)} %text.3), custom_call_target="tpu_custom_call" | custom-call | flops 4718592 | bytes 1024 | tf_op jit(solution)/shard_map/pallas_call | solution.py:196
  2.4 2.3 %shard_map.60 = (bf16[1024,1152]{1,0:T(8,128)(2,1)S(1)}, bf16[256,1152]{1,0:T(8,128)(2,1)S(1)}, bf16[1024,1152]{1,0:T(8,128)(2,1)S(1)}, bf16[1024,1152]{1,0:T(8,...) custom-call(s32[1]{0:T(128)} %bitcast.parity_ref, ...), custom_call_target="tpu_custom_call" | custom-call | flops 9437184 | bytes 1024 | tf_op jit(solution)/shard_map/pallas_call | solution.py:202
  4.6 0.1 collective-permute-start.2
  4.7 8.9 %collective-permute-start.1 = (bf16[768,1152]{1,0:T(8,128)(2,1)S(1)}, bf16[768,1152]{1,0:T(8,128)(2,1)S(1)}, u32[]{:S(2)}, u32[]{:S(2)}) collective-permute-start(bf16[768,1152]{1,0:T(8,128)(2,1)S(1)} %get-tuple-element.17.z1), channel_id=1, source_target_pairs={{0,255},{1,2},{2,1},{3,4},{4,3},{5,6},{6,5},{7,8},{8,7},{9,10},{10... | collective-permute-start | bytes 5308424 | tf_op jit(solution)/shard_map/ppermute | solution.py:201
  13.6 0.0 collective-permute-start
  14.9 5.8 %shard_map.61 = (bf16[1024,1024]{1,0:T(8,128)(2,1)S(1)}, f32[1024,1152]{1,0:T(8,128)S(1)}) custom-call(f32[1]{0:T(128)S(6)} %copy.10.multiplier_ref, f32[1]{0:T(128)S(6)} %copy.11.bias_ref, bf16[1024,1152]{1,0:T(8,128)(2,1)S(1)} %get-tuple-element.20.zp, bf16[1024,1152]{1,0:T(8,128)(2,1)S(1)} %get-tuple-element.18.zq), custom_call_target="tpu_custom_call" | custom-call | flops 75497472 | bytes 1024 | tf_op jit(solution)/shard_map/pallas_call | solution.py:212
  20.8 0.0 collective-permute-done.2.other
  20.8 10.1 %shard_map.62 = (bf16[1024,1152]{1,0:T(8,128)(2,1)}, bf16[1024,1152]{1,0:T(8,128)(2,1)}, f32[8,128]{1,0:T(8,128)S(1)}) custom-call(s32[1]{0:T(128)} %bitcast.parity_ref, f32[1]{0:T(128)S(6)} %copy.10.multiplier_ref, f32[1]{0:T(128)S(6)} %copy.11.bias_ref, bf16[1024,1152]{1,0:T(8,128)(2,1)S(1)} %get-tuple-element.20.zp, ...), custom_call_target="tpu_custom_call" | custom-call | flops 113246208 | bytes 1024 | tf_op jit(solution)/shard_map/pallas_call | solution.py:217
  30.9 2.9 %collective-permute-done.1.other = bf16[768,1152]{1,0:T(8,128)(2,1)S(1)} collective-permute-done((bf16[768,1152]{1,0:T(8,128)(2,1)S(1)}, bf16[768,1152]{1,0:T(8,128)(2,1)S(1)}, u32[]{:S(2)}, u32[]{:S(2)}) %collective-permute-start.1) | collective-permute-done | bytes 1769504 | tf_op jit(solution)/shard_map/ppermute | solution.py:201
  33.8 4.7 %shard_map.63.gq = f32[1024,1152]{1,0:T(8,128)S(1)} custom-call(f32[1]{0:T(128)S(6)} %copy.10.multiplier_ref, f32[1]{0:T(128)S(6)} %copy.11.bias_ref, bf16[1024,1152]{1,0:T(8,128)(2,1)S(1)} %get-tuple-element.18.zq, bf16[768,1152]{1,0:T(8,128)(2,1)S(1)} %collective-permute-done.1.other, f32[1024,1152]{1,0:T(8,128)S(1)} %get-tuple-element.21.gq, ...), custom_call_target="tpu_custom_call" | custom-call | flops 56623104 | bytes 1024 | tf_op jit(solution)/shard_map/pallas_call | solution.py:223
  38.5 1.6 %collective-permute-done.other = bf16[256,1152]{1,0:T(8,128)(2,1)S(1)} collective-permute-done((bf16[256,1152]{1,0:T(8,128)(2,1)S(1)}, bf16[256,1152]{1,0:T(8,128)(2,1)S(1)}, u32[]{:S(2)}, u32[]{:S(2)}) %collective-permute-start) | collective-permute-done | bytes 589856 | tf_op jit(solution)/shard_map/ppermute | solution.py:211
  40.1 4.2 %shard_map.64 = (bf16[1024,1152]{1,0:T(8,128)(2,1)}, bf16[1024,1152]{1,0:T(8,128)(2,1)}) custom-call(s32[1]{0:T(128)} %bitcast.parity_ref, f32[1]{0:T(128)S(6)} %copy.10.multiplier_ref, f32[1]{0:T(128)S(6)} %copy.11.bias_ref, bf16[1024,1152]{1,0:T(8,128)(2,1)S(1)} %get-tuple-element.18.zq, ...), custom_call_target="tpu_custom_call", output_to_operand_aliasing={{0}: (10, {}), {1}: (11, {})} | custom-call | flops 18874368 | bytes 1024 | tf_op jit(solution)/shard_map/pallas_call | solution.py:227
Async XLA Ops:
  4.6 16.1 %collective-permute-start.2 = (bf16[1024,1152]{1,0:T(8,128)(2,1)S(1)}, bf16[1024,1152]{1,0:T(8,128)(2,1)S(1)}, u32[]{:S(2)}, u32[]{:S(2)}) collective-permute-start(bf16[1024,1152]{1,0:T(8,128)(2,1)S(1)} %get-tuple-element.20.zp), channel_id=1, source_target_pairs={{0,1},{1,0},{2,3},{3,2},{4,5},{5,4},{6,7},{7,6},{8,9},{9,8},{10,11... | collective-permute-start | bytes 7077896 | tf_op jit(solution)/shard_map/ppermute | solution.py:210
  4.7 29.1 %collective-permute-start.1 = (bf16[768,1152]{1,0:T(8,128)(2,1)S(1)}, bf16[768,1152]{1,0:T(8,128)(2,1)S(1)}, u32[]{:S(2)}, u32[]{:S(2)}) collective-permute-start(bf16[768,1152]{1,0:T(8,128)(2,1)S(1)} %get-tuple-element.17.z1), channel_id=1, source_target_pairs={{0,255},{1,2},{2,1},{3,4},{4,3},{5,6},{6,5},{7,8},{8,7},{9,10},{10... | collective-permute-start | bytes 5308424 | tf_op jit(solution)/shard_map/ppermute | solution.py:201
  13.6 26.5 %collective-permute-start = (bf16[256,1152]{1,0:T(8,128)(2,1)S(1)}, bf16[256,1152]{1,0:T(8,128)(2,1)S(1)}, u32[]{:S(2)}, u32[]{:S(2)}) collective-permute-start(bf16[256,1152]{1,0:T(8,128)(2,1)S(1)} %get-tuple-element.19), channel_id=1, source_target_pairs={{0,255},{1,2},{2,1},{3,4},{4,3},{5,6},{6,5},{7,8},{8,7},{9,10},{10... | collective-permute-start | bytes 1769480 | tf_op jit(solution)/shard_map/ppermute | solution.py:211

commit v2 on v1

--- a/solution.py
+++ b/solution.py
@@ -176,7 +176,7 @@
         out_specs=out_specs,
         scratch_shapes=scratch,
         compiler_params=pltpu.CompilerParams(vmem_limit_bytes=limit * MIB),
-        cost_estimate=pl.CostEstimate(flops=flops // 64, bytes_accessed=1024, transcendentals=0),
+        cost_estimate=pl.CostEstimate(flops=flops * 16 if kernel in (first_kernel, rest_kernel, local_kernel) else flops, bytes_accessed=flops, transcendentals=0),
         **more,
     )
 

time: 44.7 us -> 43 us (0.962)
  the two profiles are of different devices: /device:TPU:0 before, /device:TPU:1 now
where the time goes in v2:
time: 43 us; the launch traced here: 42.8 us
  Pallas kernels  28.7 us (67%)
  starting transfers between devices  11.9 us (28%)
  between operations  2.18 us (5%)
    pallas_call x1, Pallas kernels, on_device(): call(near_kernel, (pltpu.HBM((rows, width), BF16),) * 2 + (shape(8, 128,...  10.1 us
    ppermute x1, starting transfers between devices, on_device(): near_block = lax.ppermute(zp, 'dp', near)  9.1 us
    pallas_call x1, Pallas kernels, on_device(): call(local_kernel, (shape(rows, rows, BF16), shape(rows, width, F32)), [S...  5.84 us
    pallas_call x1, Pallas kernels, on_device(): call(far_kernel, shape(rows, width, F32), [SMEM, SMEM, VMEM, VMEM, VMEM,...  4.63 us
    pallas_call x1, Pallas kernels, on_device(): call(last_kernel, (pltpu.HBM((rows, width), BF16),) * 2, [SMEM] * 3 + [VM...  4.21 us
    ppermute x1, starting transfers between devices, on_device(): far1 = lax.ppermute(z1, 'dp', far)  2.69 us
    pallas_call x1, Pallas kernels, on_device(): call(rest_kernel, (shape(rows, width, BF16), shape(rest, width, BF16), sh...  2.26 us
    pallas_call x1, Pallas kernels, on_device(): call(first_kernel, (shape(first, width, BF16), shape(first, width, BF16),...  1.7 us
  transfers between devices with their start and end apart: 3, of which 0 were waited for; matrix products, arithmetic and copies ran while one was open for 0% of the time, Pallas kernels for 53%

profile of v2, /device:TPU:1, one launch (start us, length us, event | category | flops | bytes accessed | tf_op | source)
XLA Modules:
  0.0 42.8 jit_solution(8725223384774040247)
XLA Ops:
  0.6 1.7 %shard_map.59 = (bf16[768,1152]{1,0:T(8,128)(2,1)S(1)}, bf16[768,1152]{1,0:T(8,128)(2,1)S(1)}, f32[768,1]{1,0:T(8,128)S(1)}) custom-call(s32[1]{0:T(128)} %bitcast.parity_ref, bf16[1024,1152]{1,0:T(8,128)(2,1)} %image.3, bf16[1024,1152]{1,0:T(8,128)(2,1)} %text.3), custom_call_target="tpu_custom_call" | custom-call | flops 4831838208 | bytes 301989888 | tf_op jit(solution)/shard_map/pallas_call | solution.py:196
  2.4 2.7 %collective-permute-start.1 = (bf16[768,1152]{1,0:T(8,128)(2,1)S(1)}, bf16[768,1152]{1,0:T(8,128)(2,1)S(1)}, u32[]{:S(2)}, u32[]{:S(2)}) collective-permute-start(bf16[768,1152]{1,0:T(8,128)(2,1)S(1)} %get-tuple-element.17.z1), channel_id=1, source_target_pairs={{0,255},{1,2},{2,1},{3,4},{4,3},{5,6},{6,5},{7,8},{8,7},{9,10},{10... | collective-permute-start | bytes 5308424 | tf_op jit(solution)/shard_map/ppermute | solution.py:201
  5.0 2.3 %shard_map.60 = (bf16[1024,1152]{1,0:T(8,128)(2,1)S(1)}, bf16[256,1152]{1,0:T(8,128)(2,1)S(1)}, bf16[1024,1152]{1,0:T(8,128)(2,1)S(1)}, bf16[1024,1152]{1,0:T(8,...) custom-call(s32[1]{0:T(128)} %bitcast.parity_ref, ...), custom_call_target="tpu_custom_call" | custom-call | flops 9663676416 | bytes 603979776 | tf_op jit(solution)/shard_map/pallas_call | solution.py:202
  7.3 0.1 collective-permute-start
  7.4 9.1 %collective-permute-start.2 = (bf16[1024,1152]{1,0:T(8,128)(2,1)S(1)}, bf16[1024,1152]{1,0:T(8,128)(2,1)S(1)}, u32[]{:S(2)}, u32[]{:S(2)}) collective-permute-start(bf16[1024,1152]{1,0:T(8,128)(2,1)S(1)} %get-tuple-element.20.zp), channel_id=1, source_target_pairs={{0,1},{1,0},{2,3},{3,2},{4,5},{5,4},{6,7},{7,6},{8,9},{9,8},{10,11... | collective-permute-start | bytes 7077896 | tf_op jit(solution)/shard_map/ppermute | solution.py:210
  17.8 5.8 %shard_map.61 = (bf16[1024,1024]{1,0:T(8,128)(2,1)S(1)}, f32[1024,1152]{1,0:T(8,128)S(1)}) custom-call(f32[1]{0:T(128)S(6)} %copy.10.multiplier_ref, f32[1]{0:T(128)S(6)} %copy.11.bias_ref, bf16[1024,1152]{1,0:T(8,128)(2,1)S(1)} %get-tuple-element.20.zp, bf16[1024,1152]{1,0:T(8,128)(2,1)S(1)} %get-tuple-element.18.zq), custom_call_target="tpu_custom_call" | custom-call | flops 77309411328 | bytes 4831838208 | tf_op jit(solution)/shard_map/pallas_call | solution.py:212
  23.7 0.0 collective-permute-done.2.other
  23.7 10.1 %shard_map.62 = (bf16[1024,1152]{1,0:T(8,128)(2,1)}, bf16[1024,1152]{1,0:T(8,128)(2,1)}, f32[8,128]{1,0:T(8,128)S(1)}) custom-call(s32[1]{0:T(128)} %bitcast.parity_ref, f32[1]{0:T(128)S(6)} %copy.10.multiplier_ref, f32[1]{0:T(128)S(6)} %copy.11.bias_ref, bf16[1024,1152]{1,0:T(8,128)(2,1)S(1)} %get-tuple-element.20.zp, ...), custom_call_target="tpu_custom_call" | custom-call | flops 7247757312 | bytes 7247757312 | tf_op jit(solution)/shard_map/pallas_call | solution.py:217
  33.8 0.0 collective-permute-done.1.other
  33.8 4.6 %shard_map.63.gq = f32[1024,1152]{1,0:T(8,128)S(1)} custom-call(f32[1]{0:T(128)S(6)} %copy.10.multiplier_ref, f32[1]{0:T(128)S(6)} %copy.11.bias_ref, bf16[1024,1152]{1,0:T(8,128)(2,1)S(1)} %get-tuple-element.18.zq, bf16[768,1152]{1,0:T(8,128)(2,1)S(1)} %collective-permute-done.1.other, f32[1024,1152]{1,0:T(8,128)S(1)} %get-tuple-element.21.gq, ...), custom_call_target="tpu_custom_call" | custom-call | flops 3623878656 | bytes 3623878656 | tf_op jit(solution)/shard_map/pallas_call | solution.py:223
  38.4 0.0 collective-permute-done.other
  38.4 4.2 %shard_map.64 = (bf16[1024,1152]{1,0:T(8,128)(2,1)}, bf16[1024,1152]{1,0:T(8,128)(2,1)}) custom-call(s32[1]{0:T(128)} %bitcast.parity_ref, f32[1]{0:T(128)S(6)} %copy.10.multiplier_ref, f32[1]{0:T(128)S(6)} %copy.11.bias_ref, bf16[1024,1152]{1,0:T(8,128)(2,1)S(1)} %get-tuple-element.18.zq, ...), custom_call_target="tpu_custom_call", output_to_operand_aliasing={{0}: (10, {}), {1}: (11, {})} | custom-call | flops 1207959552 | bytes 1207959552 | tf_op jit(solution)/shard_map/pallas_call | solution.py:227
Async XLA Ops:
  2.4 31.4 %collective-permute-start.1 = (bf16[768,1152]{1,0:T(8,128)(2,1)S(1)}, bf16[768,1152]{1,0:T(8,128)(2,1)S(1)}, u32[]{:S(2)}, u32[]{:S(2)}) collective-permute-start(bf16[768,1152]{1,0:T(8,128)(2,1)S(1)} %get-tuple-element.17.z1), channel_id=1, source_target_pairs={{0,255},{1,2},{2,1},{3,4},{4,3},{5,6},{6,5},{7,8},{8,7},{9,10},{10... | collective-permute-start | bytes 5308424 | tf_op jit(solution)/shard_map/ppermute | solution.py:201
  7.3 31.1 %collective-permute-start = (bf16[256,1152]{1,0:T(8,128)(2,1)S(1)}, bf16[256,1152]{1,0:T(8,128)(2,1)S(1)}, u32[]{:S(2)}, u32[]{:S(2)}) collective-permute-start(bf16[256,1152]{1,0:T(8,128)(2,1)S(1)} %get-tuple-element.19), channel_id=1, source_target_pairs={{0,255},{1,2},{2,1},{3,4},{4,3},{5,6},{6,5},{7,8},{8,7},{9,10},{10... | collective-permute-start | bytes 1769480 | tf_op jit(solution)/shard_map/ppermute | solution.py:211
  7.4 16.2 %collective-permute-start.2 = (bf16[1024,1152]{1,0:T(8,128)(2,1)S(1)}, bf16[1024,1152]{1,0:T(8,128)(2,1)S(1)}, u32[]{:S(2)}, u32[]{:S(2)}) collective-permute-start(bf16[1024,1152]{1,0:T(8,128)(2,1)S(1)} %get-tuple-element.20.zp), channel_id=1, source_target_pairs={{0,1},{1,0},{2,3},{3,2},{4,5},{5,4},{6,7},{7,6},{8,9},{9,8},{10,11... | collective-permute-start | bytes 7077896 | tf_op jit(solution)/shard_map/ppermute | solution.py:210

commit v3 on v2

v3 whole, which is shorter than its diff:
```python
import functools

import jax
import jax.numpy as jnp
from jax import lax
from jax.experimental import pallas as pl
from jax.experimental.pallas import tpu as pltpu
from jax.sharding import PartitionSpec as P

epsilon = 1e-06
LOG2_E = 1.4426950408889634
F32, BF16 = jnp.float32, jnp.bfloat16
BLOCK = 256
FIRST = 768
MIB = 2**20

VMEM = pl.BlockSpec(memory_space=pltpu.VMEM)
SMEM = pl.BlockSpec(memory_space=pltpu.SMEM)
HBM = pl.BlockSpec(memory_space=pl.ANY)


def rows_dot_rows(a, b):
    return lax.dot_general(a, b, (((1,), (1,)), ((), ())), preferred_element_type=F32)


def columns_dot(a, b):
    return lax.dot_general(a, b, (((0,), (0,)), ((), ())), preferred_element_type=F32)


def dot(a, b):
    return jnp.dot(a, b, preferred_element_type=F32)


def blocks(rows):
    return [slice(start, start + BLOCK) for start in range(0, rows, BLOCK)]


def fetch(parity, if_even, if_odd, start, target, sems):
    for i, here in enumerate(blocks(target.shape[0])):
        there = pl.ds(start + here.start, BLOCK)

        @pl.when(parity == 0)
        def _():
            pltpu.make_async_copy(if_even.at[there], target.at[here], sems.at[i]).start()

        @pl.when(parity == 1)
        def _():
            pltpu.make_async_copy(if_odd.at[there], target.at[here], sems.at[i]).start()


def arrived(source, target, sems, i, here):
    pltpu.make_async_copy(source.at[pl.ds(0, BLOCK)], target.at[here], sems.at[i]).wait()


def normalize_block(raw):
    floats = raw.astype(F32)
    inverse = lax.rsqrt(jnp.sum(floats * floats, axis=-1, keepdims=True) + epsilon)
    return (floats * inverse).astype(BF16), inverse


def my_parity():
    return lax.rem(lax.axis_index("dp"), 2)


def first_kernel(image, text, z1, raw1, inv1, sems):
    fetch(my_parity(), image, text, 0, raw1, sems)
    for i, here in enumerate(blocks(raw1.shape[0])):
        arrived(image, raw1, sems, i, here)
        z1[here, :], inv1[here, :] = normalize_block(raw1[here, :])


def rest_kernel(
    image, text, multiplier, bias, z1, zp, z2, zq, rawp, raw2, invp, inv2, consts, semsp, sems2
):
    first = z1.shape[0]
    parity = my_parity()
    fetch(parity, text, image, 0, rawp, semsp)
    fetch(parity, image, text, first, raw2, sems2)
    consts[0:1, :] = jnp.broadcast_to(multiplier[...], (1, consts.shape[1]))
    consts[1:2, :] = jnp.broadcast_to(bias[...], (1, consts.shape[1]))
    zq[:first, :] = z1[...]
    for i, here in enumerate(blocks(rawp.shape[0])):
        arrived(image, rawp, semsp, i, here)
        zp[here, :], invp[here, :] = normalize_block(rawp[here, :])
    for i, here in enumerate(blocks(raw2.shape[0])):
        arrived(image, raw2, sems2, i, here)
        normed, inv2[here, :] = normalize_block(raw2[here, :])
        z2[here, :] = normed
        zq[pl.ds(first + here.start, BLOCK), :] = normed


def constants(consts):
    multiplier, bias = consts[0:1, 0:1], consts[1:2, 0:1]
    return multiplier, -multiplier * LOG2_E, -bias * LOG2_E


def exponential(agreement, scale, shift):
    return jnp.exp2(agreement * scale + shift)


def local_kernel(consts, zp, zq, coef, gq):
    multiplier, scale, shift = constants(consts)
    count = zq.shape[0]
    for here in blocks(zp.shape[0]):
        power = exponential(rows_dot_rows(zp[here, :], zq[...]), scale, shift)
        value = multiplier / (1.0 + power)
        row = lax.broadcasted_iota(jnp.int32, (BLOCK, count), 0) + here.start
        column = lax.broadcasted_iota(jnp.int32, (BLOCK, count), 1)
        coef[here, :] = jnp.where(row == column, -power * value, value).astype(BF16)
    for here in blocks(count):
        gq[here, :] = columns_dot(coef[:, here], zp[...])


def backward(raw, inverse, upstream):
    floats = raw.astype(F32)
    inner = jnp.sum(floats * upstream, axis=-1, keepdims=True)
    return inverse * (upstream - floats * (inverse * inverse * inner))


def near_kernel(consts, zp, zq, coef, other, rawp, invp, grad):
    multiplier, scale, shift = constants(consts)
    for here in blocks(zp.shape[0]):
        total = dot(coef[here, :], zq[...])
        power = exponential(rows_dot_rows(zp[here, :], other[...]), scale, shift)
        factors = (multiplier / (1.0 + power)).astype(BF16)
        total = total + dot(factors, other[...])
        grad[here, :] = backward(rawp[here, :], invp[here, :], total).astype(BF16)


def put(parity, if_even, if_odd, there, source, sem):
    @pl.when(parity == 0)
    def _():
        pltpu.make_async_copy(source, if_even.at[there], sem).start()

    @pl.when(parity == 1)
    def _():
        pltpu.make_async_copy(source, if_odd.at[there], sem).start()


def raw_block(here, raw1, raw2, inv1, inv2):
    first = raw1.shape[0]
    if here.start < first:
        return raw1[here, :], inv1[here, :]
    there = slice(here.start - first, here.stop - first)
    return raw2[there, :], inv2[there, :]


def far_kernel(
    consts, zq, other, gq, raw1, raw2, inv1, inv2, after_near, so_far
):
    multiplier, scale, shift = constants(consts)
    for here in blocks(zq.shape[0]):
        power = exponential(rows_dot_rows(zq[here, :], other[...]), scale, shift)
        factors = (multiplier / (1.0 + power)).astype(BF16)
        total = gq[here, :] + dot(factors, other[...])
        so_far[here, :] = backward(*raw_block(here, raw1, raw2, inv1, inv2), total)


def last_kernel(
    consts, zq, other, so_far, raw1, raw2, inv1, inv2, grad, image_out, text_out, held, sems, grad_sem
):
    multiplier, scale, shift = constants(consts)
    parity = my_parity()
    everything = pl.ds(0, grad.shape[0])
    put(parity, text_out, image_out, everything, grad, grad_sem)
    pieces = blocks(zq.shape[0])
    ahead = rows_dot_rows(zq[pieces[0], :], other[...])
    for i, here in enumerate(pieces):
        agreement = ahead
        if i + 1 < len(pieces):
            ahead = rows_dot_rows(zq[pieces[i + 1], :], other[...])
        factors = multiplier / (1.0 + exponential(agreement, scale, shift))
        inner = jnp.sum(factors * agreement, axis=-1, keepdims=True)
        term = dot(factors.astype(BF16), other[...])
        raw, inverse = raw_block(here, raw1, raw2, inv1, inv2)
        more = inverse * term - raw.astype(F32) * (inverse * inverse * inner)
        held[here, :] = (so_far[here, :] + more).astype(BF16)
        put(parity, image_out, text_out, here, held.at[here], sems.at[i])
    pltpu.make_async_copy(grad, image_out.at[everything], grad_sem).wait()
    for i, here in enumerate(pieces):
        pltpu.make_async_copy(held.at[here], image_out.at[here], sems.at[i]).wait()


def shape(rows, columns, kind):
    return jax.ShapeDtypeStruct((rows, columns), kind)


def call(kernel, out_shape, in_specs, out_specs, scratch, limit, flops, weight=1, **more):
    return pl.pallas_call(
        kernel,
        out_shape=out_shape,
        in_specs=in_specs,
        out_specs=out_specs,
        scratch_shapes=scratch,
        compiler_params=pltpu.CompilerParams(vmem_limit_bytes=limit * MIB),
        cost_estimate=pl.CostEstimate(
            flops=flops * weight, bytes_accessed=flops, transcendentals=0
        ),
        **more,
    )


def on_device(image_emb, text_emb, cosine_multiplier, logit_bias):
    rows, width = image_emb.shape
    count = lax.axis_size("dp")
    near = [(e, e ^ 1) for e in range(count)]
    far = [(e, (e - 1) % count if e % 2 == 0 else (e + 1) % count) for e in range(count)]
    first, rest = FIRST, rows - FIRST
    image_emb = pltpu.with_memory_space_constraint(image_emb, pltpu.HBM)
    text_emb = pltpu.with_memory_space_constraint(text_emb, pltpu.HBM)
    dma = pltpu.SemaphoreType.DMA
    product = 2 * rows * rows * width

    z1, raw1, inv1 = call(
        first_kernel,
        (shape(first, width, BF16), shape(first, width, BF16), shape(first, 1, F32)),
        [HBM, HBM], (VMEM,) * 3, [dma((first // BLOCK,))], 4, product // 8, 16,
    )(image_emb, text_emb)
    far1 = lax.ppermute(z1, "dp", far)
    zp, z2, zq, rawp, raw2, invp, inv2, consts = call(
        rest_kernel,
        (
            shape(rows, width, BF16), shape(rest, width, BF16), shape(rows, width, BF16),
            shape(rows, width, BF16), shape(rest, width, BF16), shape(rows, 1, F32), shape(rest, 1, F32),
            shape(8, 128, F32),
        ),
        [HBM] * 2 + [VMEM] * 3, (VMEM,) * 8,
        [dma((rows // BLOCK,)), dma((rest // BLOCK,))], 4, product // 4, 16,
    )(image_emb, text_emb, cosine_multiplier.reshape(1, 1), logit_bias.reshape(1, 1), z1)
    near_block = lax.ppermute(zp, "dp", near)
    far2 = lax.ppermute(z2, "dp", far)
    coef, gq = call(
        local_kernel,
        (shape(rows, rows, BF16), shape(rows, width, F32)),
        [VMEM] * 3, (VMEM,) * 2, [], 8, 2 * product, 16,
    )(consts, zp, zq)
    grad = call(
        near_kernel, shape(rows, width, BF16),
        [VMEM] * 7, VMEM, [], 12, 3 * product,
    )(consts, zp, zq, coef, near_block, rawp, invp)
    so_far = call(
        far_kernel, shape(rows, width, F32),
        [VMEM] * 9, VMEM, [], 8, 2 * product * first // rows,
    )(consts, zq, far1, gq, raw1, raw2, inv1, inv2, grad)
    return call(
        last_kernel,
        (pltpu.HBM((rows, width), BF16),) * 2,
        [VMEM] * 9, (HBM, HBM),
        [pltpu.VMEM((rows, width), BF16), dma((rows // BLOCK,)), dma], 12, 2 * product * rest // rows,
    )(consts, zq, far2, so_far, raw1, raw2, inv1, inv2, grad)


def solution(mesh):
    in_specs = (P("dp", None), P("dp", None), P(), P())
    out_specs = (P("dp", None), P("dp", None))
    return jax.shard_map(
        on_device, mesh=mesh, in_specs=in_specs, out_specs=out_specs, check_vma=False
    )
```

time: 43 us -> 41.7 us (0.970)
  Pallas kernels: 28.7 us -> 27.5 us
    pallas_call x4, Pallas kernels: 24.8 us -> 23.7 us  [the longest x1 9.18 us: on_device(): call(near_kernel, shape(rows, width, BF16), [VMEM] * 7, VMEM, [], 12, 3 *...]
  transfers between devices with their start and end apart: 3 -> 3, of which waited for: 0 -> 0; matrix products, arithmetic and copies ran while one was open for 0% -> 0% of each run, Pallas kernels for 53% -> 55%
where the time goes in v3:
time: 41.7 us; the launch traced here: 41.6 us
  Pallas kernels  27.5 us (66%)
  starting transfers between devices  11.9 us (29%)
  between operations  2.17 us (5%)
    pallas_call x1, Pallas kernels, on_device(): call(near_kernel, shape(rows, width, BF16), [VMEM] * 7, VMEM, [], 12, 3 *...  9.18 us
    ppermute x1, starting transfers between devices, on_device(): near_block = lax.ppermute(zp, 'dp', near)  9.11 us
    pallas_call x1, Pallas kernels, on_device(): call(local_kernel, (shape(rows, rows, BF16), shape(rows, width, F32)), [V...  5.79 us
    pallas_call x1, Pallas kernels, on_device(): call(far_kernel, shape(rows, width, F32), [VMEM] * 9, VMEM, [], 8, 2 * pr...  5.58 us
    pallas_call x1, Pallas kernels, on_device(): call(last_kernel, (pltpu.HBM((rows, width), BF16),) * 2, [VMEM] * 9, (HBM...  3.11 us
    ppermute x1, starting transfers between devices, on_device(): far1 = lax.ppermute(z1, 'dp', far)  2.69 us
    pallas_call x1, Pallas kernels, on_device(): call(rest_kernel, (shape(rows, width, BF16), shape(rest, width, BF16), sh...  2.15 us
    pallas_call x1, Pallas kernels, on_device(): call(first_kernel, (shape(first, width, BF16), shape(first, width, BF16),...  1.71 us
  transfers between devices with their start and end apart: 3, of which 0 were waited for; matrix products, arithmetic and copies ran while one was open for 0% of the time, Pallas kernels for 55%

profile of v3, /device:TPU:1, one launch (start us, length us, event | category | flops | bytes accessed | tf_op | source)
XLA Modules:
  0.0 41.6 jit_solution(13197827947607600987)
XLA Ops:
  0.6 1.7 %shard_map.59 = (bf16[768,1152]{1,0:T(8,128)(2,1)S(1)}, bf16[768,1152]{1,0:T(8,128)(2,1)S(1)}, f32[768,1]{1,0:T(8,128)S(1)}) custom-call(bf16[1024,1152]{1,0:T(8,128)(2,1)} %image.3, bf16[1024,1152]{1,0:T(8,128)(2,1)} %text.3), custom_call_target="tpu_custom_call" | custom-call | flops 4831838208 | bytes 301989888 | tf_op jit(solution)/shard_map/pallas_call | solution.py:214
  2.3 2.7 %collective-permute-start.1 = (bf16[768,1152]{1,0:T(8,128)(2,1)S(1)}, bf16[768,1152]{1,0:T(8,128)(2,1)S(1)}, u32[]{:S(2)}, u32[]{:S(2)}) collective-permute-start(bf16[768,1152]{1,0:T(8,128)(2,1)S(1)} %get-tuple-element.15.z1), channel_id=1, source_target_pairs={{0,255},{1,2},{2,1},{3,4},{4,3},{5,6},{6,5},{7,8},{8,7},{9,10},{10... | collective-permute-start | bytes 5308424 | tf_op jit(solution)/shard_map/ppermute | solution.py:219
  6.3 2.1 %shard_map.60 = (bf16[1024,1152]{1,0:T(8,128)(2,1)S(1)}, bf16[256,1152]{1,0:T(8,128)(2,1)S(1)}, bf16[1024,1152]{1,0:T(8,128)(2,1)S(1)}, bf16[1024,1152]{1,0:T(8,...) custom-call(bf16[1024,1152]{1,0:T(8,128)(2,1)} %image.3, ...), custom_call_target="tpu_custom_call" | custom-call | flops 9663676416 | bytes 603979776 | tf_op jit(solution)/shard_map/pallas_call | solution.py:220
  8.5 0.1 collective-permute-start
  8.6 9.1 %collective-permute-start.2 = (bf16[1024,1152]{1,0:T(8,128)(2,1)S(1)}, bf16[1024,1152]{1,0:T(8,128)(2,1)S(1)}, u32[]{:S(2)}, u32[]{:S(2)}) collective-permute-start(bf16[1024,1152]{1,0:T(8,128)(2,1)S(1)} %get-tuple-element.19.zp), channel_id=1, source_target_pairs={{0,1},{1,0},{2,3},{3,2},{4,5},{5,4},{6,7},{7,6},{8,9},{9,8},{10,11... | collective-permute-start | bytes 7077896 | tf_op jit(solution)/shard_map/ppermute | solution.py:230
  17.7 5.8 %shard_map.61 = (bf16[1024,1024]{1,0:T(8,128)(2,1)S(1)}, f32[1024,1152]{1,0:T(8,128)S(1)}) custom-call(f32[8,128]{1,0:T(8,128)S(1)} %get-tuple-element.16.consts, bf16[1024,1152]{1,0:T(8,128)(2,1)S(1)} %get-tuple-element.19.zp, bf16[1024,1152]{1,0:T(8,128)(2,1)S(1)} %get-tuple-element.17.zq), custom_call_target="tpu_custom_call" | custom-call | flops 77309411328 | bytes 4831838208 | tf_op jit(solution)/shard_map/pallas_call | solution.py:232
  23.5 0.0 collective-permute-done.2.other
  23.5 9.2 %shard_map.62.after_near.grad = bf16[1024,1152]{1,0:T(8,128)(2,1)S(1)} custom-call(f32[8,128]{1,0:T(8,128)S(1)} %get-tuple-element.16.consts, bf16[1024,1152]{1,0:T(8,128)(2,1)S(1)} %get-tuple-element.19.zp, bf16[1024,1152]{1,0:T(8,128)(2,1)S(1)} %get-tuple-element.17.zq, bf16[1024,1024]{1,0:T(8,128)(2,1)S(1)} %get-tuple-element.25.coef, ...), custom_call_target="tpu_custom_call" | custom-call | flops 7247757312 | bytes 7247757312 | tf_op jit(solution)/shard_map/pallas_call | solution.py:237
  32.7 0.0 collective-permute-done.1.other
  32.7 5.6 %shard_map.63.so_far = f32[1024,1152]{1,0:T(8,128)S(1)} custom-call(f32[8,128]{1,0:T(8,128)S(1)} %get-tuple-element.16.consts, bf16[1024,1152]{1,0:T(8,128)(2,1)S(1)} %get-tuple-element.17.zq, bf16[768,1152]{1,0:T(8,128)(2,1)S(1)} %collective-permute-done.1.other, f32[1024,1152]{1,0:T(8,128)S(1)} %get-tuple-element.20.gq, ...), custom_call_target="tpu_custom_call" | custom-call | flops 3623878656 | bytes 3623878656 | tf_op jit(solution)/shard_map/pallas_call | solution.py:241
  38.3 0.0 collective-permute-done.other
  38.3 3.1 %shard_map.64 = (bf16[1024,1152]{1,0:T(8,128)(2,1)}, bf16[1024,1152]{1,0:T(8,128)(2,1)}) custom-call(f32[8,128]{1,0:T(8,128)S(1)} %get-tuple-element.16.consts, bf16[1024,1152]{1,0:T(8,128)(2,1)S(1)} %get-tuple-element.17.zq, bf16[256,1152]{1,0:T(8,128)(2,1)S(1)} %collective-permute-done.other, f32[1024,1152]{1,0:T(8,128)S(1)} %shard_map.63.so_far, ...), custom_call_target="tpu_custom_call" | custom-call | flops 1207959552 | bytes 1207959552 | tf_op jit(solution)/shard_map/pallas_call | solution.py:245
Async XLA Ops:
  2.3 30.4 %collective-permute-start.1 = (bf16[768,1152]{1,0:T(8,128)(2,1)S(1)}, bf16[768,1152]{1,0:T(8,128)(2,1)S(1)}, u32[]{:S(2)}, u32[]{:S(2)}) collective-permute-start(bf16[768,1152]{1,0:T(8,128)(2,1)S(1)} %get-tuple-element.15.z1), channel_id=1, source_target_pairs={{0,255},{1,2},{2,1},{3,4},{4,3},{5,6},{6,5},{7,8},{8,7},{9,10},{10... | collective-permute-start | bytes 5308424 | tf_op jit(solution)/shard_map/ppermute | solution.py:219
  8.5 29.8 %collective-permute-start = (bf16[256,1152]{1,0:T(8,128)(2,1)S(1)}, bf16[256,1152]{1,0:T(8,128)(2,1)S(1)}, u32[]{:S(2)}, u32[]{:S(2)}) collective-permute-start(bf16[256,1152]{1,0:T(8,128)(2,1)S(1)} %get-tuple-element.18), channel_id=1, source_target_pairs={{0,255},{1,2},{2,1},{3,4},{4,3},{5,6},{6,5},{7,8},{8,7},{9,10},{10... | collective-permute-start | bytes 1769480 | tf_op jit(solution)/shard_map/ppermute | solution.py:231
  8.6 14.9 %collective-permute-start.2 = (bf16[1024,1152]{1,0:T(8,128)(2,1)S(1)}, bf16[1024,1152]{1,0:T(8,128)(2,1)S(1)}, u32[]{:S(2)}, u32[]{:S(2)}) collective-permute-start(bf16[1024,1152]{1,0:T(8,128)(2,1)S(1)} %get-tuple-element.19.zp), channel_id=1, source_target_pairs={{0,1},{1,0},{2,3},{3,2},{4,5},{5,4},{6,7},{7,6},{8,9},{9,8},{10,11... | collective-permute-start | bytes 7077896 | tf_op jit(solution)/shard_map/ppermute | solution.py:230

commit v4 on v3

--- a/solution.py
+++ b/solution.py
@@ -58,6 +58,12 @@
     return (floats * inverse).astype(BF16), inverse
 
 
+def length_ratio(normed, inverse):
+    floats = normed.astype(F32)
+    squares = jnp.sum(floats * floats, axis=-1, keepdims=True) + 1e-30
+    return 0.5 + 0.5 * (1.0 - epsilon * inverse * inverse) / squares
+
+
 def my_parity():
     return lax.rem(lax.axis_index("dp"), 2)
 
@@ -70,7 +76,7 @@
 
 
 def rest_kernel(
-    image, text, multiplier, bias, z1, zp, z2, zq, rawp, raw2, invp, inv2, consts, semsp, sems2
+    image, text, multiplier, bias, z1, inv1, zp, z2, zq, rawp, raw2, invp, inv2, consts, ratio, semsp, sems2
 ):
     first = z1.shape[0]
     parity = my_parity()
@@ -78,15 +84,19 @@
     fetch(parity, image, text, first, raw2, sems2)
     consts[0:1, :] = jnp.broadcast_to(multiplier[...], (1, consts.shape[1]))
     consts[1:2, :] = jnp.broadcast_to(bias[...], (1, consts.shape[1]))
-    zq[:first, :] = z1[...]
+    for here in blocks(first):
+        zq[here, :] = z1[here, :]
+        ratio[here, :] = length_ratio(z1[here, :], inv1[here, :])
     for i, here in enumerate(blocks(rawp.shape[0])):
         arrived(image, rawp, semsp, i, here)
         zp[here, :], invp[here, :] = normalize_block(rawp[here, :])
     for i, here in enumerate(blocks(raw2.shape[0])):
         arrived(image, raw2, sems2, i, here)
-        normed, inv2[here, :] = normalize_block(raw2[here, :])
-        z2[here, :] = normed
-        zq[pl.ds(first + here.start, BLOCK), :] = normed
+        normed, inverse = normalize_block(raw2[here, :])
+        z2[here, :], inv2[here, :] = normed, inverse
+        there = slice(first + here.start, first + here.stop)
+        zq[there, :] = normed
+        ratio[there, :] = length_ratio(normed, inverse)
 
 
 def constants(consts):
@@ -98,7 +108,7 @@
     return jnp.exp2(agreement * scale + shift)
 
 
-def local_kernel(consts, zp, zq, coef, gq):
+def local_kernel(consts, zp, zq, coef, gq, along):
     multiplier, scale, shift = constants(consts)
     count = zq.shape[0]
     for here in blocks(zp.shape[0]):
@@ -108,7 +118,9 @@
         column = lax.broadcasted_iota(jnp.int32, (BLOCK, count), 1)
         coef[here, :] = jnp.where(row == column, -power * value, value).astype(BF16)
     for here in blocks(count):
-        gq[here, :] = columns_dot(coef[:, here], zp[...])
+        total = columns_dot(coef[:, here], zp[...])
+        gq[here, :] = total
+        along[here, :] = jnp.sum(zq[here, :].astype(F32) * total, axis=-1, keepdims=True)
 
 
 def backward(raw, inverse, upstream):
@@ -145,24 +157,8 @@
     return raw2[there, :], inv2[there, :]
 
 
-def far_kernel(
-    consts, zq, other, gq, raw1, raw2, inv1, inv2, after_near, so_far
-):
+def far_terms(consts, zq, other):
     multiplier, scale, shift = constants(consts)
-    for here in blocks(zq.shape[0]):
-        power = exponential(rows_dot_rows(zq[here, :], other[...]), scale, shift)
-        factors = (multiplier / (1.0 + power)).astype(BF16)
-        total = gq[here, :] + dot(factors, other[...])
-        so_far[here, :] = backward(*raw_block(here, raw1, raw2, inv1, inv2), total)
-
-
-def last_kernel(
-    consts, zq, other, so_far, raw1, raw2, inv1, inv2, grad, image_out, text_out, held, sems, grad_sem
-):
-    multiplier, scale, shift = constants(consts)
-    parity = my_parity()
-    everything = pl.ds(0, grad.shape[0])
-    put(parity, text_out, image_out, everything, grad, grad_sem)
     pieces = blocks(zq.shape[0])
     ahead = rows_dot_rows(zq[pieces[0], :], other[...])
     for i, here in enumerate(pieces):
@@ -170,14 +166,30 @@
         if i + 1 < len(pieces):
             ahead = rows_dot_rows(zq[pieces[i + 1], :], other[...])
         factors = multiplier / (1.0 + exponential(agreement, scale, shift))
-        inner = jnp.sum(factors * agreement, axis=-1, keepdims=True)
-        term = dot(factors.astype(BF16), other[...])
+        along = jnp.sum(factors * agreement, axis=-1, keepdims=True)
+        yield i, here, dot(factors.astype(BF16), other[...]), along
+
+
+def far_kernel(consts, zq, other, gq, along_in, after_near, so_far, along_out):
+    for _, here, term, along in far_terms(consts, zq, other):
+        so_far[here, :] = gq[here, :] + term
+        along_out[here, :] = along_in[here, :] + along
+
+
+def last_kernel(
+    consts, zq, other, so_far, along_in, ratio, raw1, raw2, inv1, inv2, grad, image_out, text_out, held, sems, grad_sem
+):
+    parity = my_parity()
+    everything = pl.ds(0, grad.shape[0])
+    put(parity, text_out, image_out, everything, grad, grad_sem)
+    for i, here, term, along in far_terms(consts, zq, other):
         raw, inverse = raw_block(here, raw1, raw2, inv1, inv2)
-        more = inverse * term - raw.astype(F32) * (inverse * inverse * inner)
-        held[here, :] = (so_far[here, :] + more).astype(BF16)
+        inner = ratio[here, :] * (along_in[here, :] + along)
+        total = so_far[here, :] + term
+        held[here, :] = (inverse * total - raw.astype(F32) * (inverse * inverse * inner)).astype(BF16)
         put(parity, image_out, text_out, here, held.at[here], sems.at[i])
     pltpu.make_async_copy(grad, image_out.at[everything], grad_sem).wait()
-    for i, here in enumerate(pieces):
+    for i, here in enumerate(blocks(zq.shape[0])):
         pltpu.make_async_copy(held.at[here], image_out.at[here], sems.at[i]).wait()
 
 
@@ -217,37 +229,37 @@
         [HBM, HBM], (VMEM,) * 3, [dma((first // BLOCK,))], 4, product // 8, 16,
     )(image_emb, text_emb)
     far1 = lax.ppermute(z1, "dp", far)
-    zp, z2, zq, rawp, raw2, invp, inv2, consts = call(
+    zp, z2, zq, rawp, raw2, invp, inv2, consts, ratio = call(
         rest_kernel,
         (
             shape(rows, width, BF16), shape(rest, width, BF16), shape(rows, width, BF16),
             shape(rows, width, BF16), shape(rest, width, BF16), shape(rows, 1, F32), shape(rest, 1, F32),
-            shape(8, 128, F32),
+            shape(8, 128, F32), shape(rows, 1, F32),
         ),
-        [HBM] * 2 + [VMEM] * 3, (VMEM,) * 8,
+        [HBM] * 2 + [VMEM] * 4, (VMEM,) * 9,
         [dma((rows // BLOCK,)), dma((rest // BLOCK,))], 4, product // 4, 16,
-    )(image_emb, text_emb, cosine_multiplier.reshape(1, 1), logit_bias.reshape(1, 1), z1)
+    )(image_emb, text_emb, cosine_multiplier.reshape(1, 1), logit_bias.reshape(1, 1), z1, inv1)
     near_block = lax.ppermute(zp, "dp", near)
     far2 = lax.ppermute(z2, "dp", far)
-    coef, gq = call(
+    coef, gq, along = call(
         local_kernel,
-        (shape(rows, rows, BF16), shape(rows, width, F32)),
-        [VMEM] * 3, (VMEM,) * 2, [], 8, 2 * product, 16,
+        (shape(rows, rows, BF16), shape(rows, width, F32), shape(rows, 1, F32)),
+        [VMEM] * 3, (VMEM,) * 3, [], 8, 2 * product, 16,
     )(consts, zp, zq)
     grad = call(
         near_kernel, shape(rows, width, BF16),
         [VMEM] * 7, VMEM, [], 12, 3 * product,
     )(consts, zp, zq, coef, near_block, rawp, invp)
-    so_far = call(
-        far_kernel, shape(rows, width, F32),
-        [VMEM] * 9, VMEM, [], 8, 2 * product * first // rows,
-    )(consts, zq, far1, gq, raw1, raw2, inv1, inv2, grad)
+    so_far, along = call(
+        far_kernel, (shape(rows, width, F32), shape(rows, 1, F32)),
+        [VMEM] * 6, (VMEM,) * 2, [], 8, 2 * product * first // rows,
+    )(consts, zq, far1, gq, along, grad)
     return call(
         last_kernel,
         (pltpu.HBM((rows, width), BF16),) * 2,
-        [VMEM] * 9, (HBM, HBM),
+        [VMEM] * 11, (HBM, HBM),
         [pltpu.VMEM((rows, width), BF16), dma((rows // BLOCK,)), dma], 12, 2 * product * rest // rows,
-    )(consts, zq, far2, so_far, raw1, raw2, inv1, inv2, grad)
+    )(consts, zq, far2, so_far, along, ratio, raw1, raw2, inv1, inv2, grad)
 
 
 def solution(mesh):

time: 41.7 us -> 41.3 us (level)
    pallas_call x3, Pallas kernels: 14.5 us -> 13.7 us  [the longest x1 6.17 us: on_device(): call(local_kernel, (shape(rows, rows, BF16), shape(rows, width, F32), sha...]
  transfers between devices with their start and end apart: 3 -> 3, of which waited for: 0 -> 0; matrix products, arithmetic and copies ran while one was open for 0% -> 0% of each run, Pallas kernels for 55% -> 54%
where the time goes in v4:
time: 41.3 us; the launch traced here: 41.1 us
  Pallas kernels  27.1 us (66%)
  starting transfers between devices  11.9 us (29%)
  between operations  2.16 us (5%)
    pallas_call x1, Pallas kernels, on_device(): call(near_kernel, shape(rows, width, BF16), [VMEM] * 7, VMEM, [], 12, 3 *...  9.2 us
    ppermute x1, starting transfers between devices, on_device(): near_block = lax.ppermute(zp, 'dp', near)  9.11 us
    pallas_call x1, Pallas kernels, on_device(): call(local_kernel, (shape(rows, rows, BF16), shape(rows, width, F32), sha...  6.17 us
    pallas_call x1, Pallas kernels, on_device(): call(far_kernel, (shape(rows, width, F32), shape(rows, 1, F32)), [VMEM] *...  4.46 us
    pallas_call x1, Pallas kernels, on_device(): call(last_kernel, (pltpu.HBM((rows, width), BF16),) * 2, [VMEM] * 11, (HB...  3.07 us
    ppermute x1, starting transfers between devices, on_device(): far1 = lax.ppermute(z1, 'dp', far)  2.69 us
    pallas_call x1, Pallas kernels, on_device(): call(rest_kernel, (shape(rows, width, BF16), shape(rest, width, BF16), sh...  2.46 us
    pallas_call x1, Pallas kernels, on_device(): call(first_kernel, (shape(first, width, BF16), shape(first, width, BF16),...  1.71 us
  transfers between devices with their start and end apart: 3, of which 0 were waited for; matrix products, arithmetic and copies ran while one was open for 0% of the time, Pallas kernels for 54%

profile of v4, /device:TPU:1, one launch (start us, length us, event | category | flops | bytes accessed | tf_op | source)
XLA Modules:
  0.0 41.1 jit_solution(4764899128548927871)
XLA Ops:
  0.6 1.7 %shard_map.59 = (bf16[768,1152]{1,0:T(8,128)(2,1)S(1)}, bf16[768,1152]{1,0:T(8,128)(2,1)S(1)}, f32[768,1]{1,0:T(8,128)S(1)}) custom-call(bf16[1024,1152]{1,0:T(8,128)(2,1)} %image.3, bf16[1024,1152]{1,0:T(8,128)(2,1)} %text.3), custom_call_target="tpu_custom_call" | custom-call | flops 4831838208 | bytes 301989888 | tf_op jit(solution)/shard_map/pallas_call | solution.py:226
  2.3 2.7 %collective-permute-start.1 = (bf16[768,1152]{1,0:T(8,128)(2,1)S(1)}, bf16[768,1152]{1,0:T(8,128)(2,1)S(1)}, u32[]{:S(2)}, u32[]{:S(2)}) collective-permute-start(bf16[768,1152]{1,0:T(8,128)(2,1)S(1)} %get-tuple-element.19.z1), channel_id=1, source_target_pairs={{0,255},{1,2},{2,1},{3,4},{4,3},{5,6},{6,5},{7,8},{8,7},{9,10},{10... | collective-permute-start | bytes 5308424 | tf_op jit(solution)/shard_map/ppermute | solution.py:231
  6.3 2.5 %shard_map.60 = (bf16[1024,1152]{1,0:T(8,128)(2,1)S(1)}, bf16[256,1152]{1,0:T(8,128)(2,1)S(1)}, bf16[1024,1152]{1,0:T(8,128)(2,1)S(1)}, bf16[1024,1152]{1,0:T(8,...) custom-call(bf16[1024,1152]{1,0:T(8,128)(2,1)} %image.3, ...), custom_call_target="tpu_custom_call" | custom-call | flops 9663676416 | bytes 603979776 | tf_op jit(solution)/shard_map/pallas_call | solution.py:232
  8.8 0.1 collective-permute-start
  8.9 9.1 %collective-permute-start.2 = (bf16[1024,1152]{1,0:T(8,128)(2,1)S(1)}, bf16[1024,1152]{1,0:T(8,128)(2,1)S(1)}, u32[]{:S(2)}, u32[]{:S(2)}) collective-permute-start(bf16[1024,1152]{1,0:T(8,128)(2,1)S(1)} %get-tuple-element.24.zp), channel_id=1, source_target_pairs={{0,1},{1,0},{2,3},{3,2},{4,5},{5,4},{6,7},{7,6},{8,9},{9,8},{10,11... | collective-permute-start | bytes 7077896 | tf_op jit(solution)/shard_map/ppermute | solution.py:242
  18.0 6.2 %shard_map.61 = (bf16[1024,1024]{1,0:T(8,128)(2,1)S(1)}, f32[1024,1152]{1,0:T(8,128)S(1)}, f32[1024,1]{1,0:T(8,128)S(1)}) custom-call(f32[8,128]{1,0:T(8,128)S(1)} %get-tuple-element.21.consts, bf16[1024,1152]{1,0:T(8,128)(2,1)S(1)} %get-tuple-element.24.zp, bf16[1024,1152]{1,0:T(8,128)(2,1)S(1)} %get-tuple-element.22.zq), custom_call_target="tpu_custom_call" | custom-call | flops 77309411328 | bytes 4831838208 | tf_op jit(solution)/shard_map/pallas_call | solution.py:244
  24.2 0.0 collective-permute-done.2.other
  24.2 9.2 %shard_map.62.after_near.grad = bf16[1024,1152]{1,0:T(8,128)(2,1)S(1)} custom-call(f32[8,128]{1,0:T(8,128)S(1)} %get-tuple-element.21.consts, bf16[1024,1152]{1,0:T(8,128)(2,1)S(1)} %get-tuple-element.24.zp, bf16[1024,1152]{1,0:T(8,128)(2,1)S(1)} %get-tuple-element.22.zq, bf16[1024,1024]{1,0:T(8,128)(2,1)S(1)} %get-tuple-element.27.coef, ...), custom_call_target="tpu_custom_call" | custom-call | flops 7247757312 | bytes 7247757312 | tf_op jit(solution)/shard_map/pallas_call | solution.py:249
  33.4 0.0 collective-permute-done.1.other
  33.4 4.5 %shard_map.63 = (f32[1024,1152]{1,0:T(8,128)S(1)}, f32[1024,1]{1,0:T(8,128)S(1)}) custom-call(f32[8,128]{1,0:T(8,128)S(1)} %get-tuple-element.21.consts, bf16[1024,1152]{1,0:T(8,128)(2,1)S(1)} %get-tuple-element.22.zq, bf16[768,1152]{1,0:T(8,128)(2,1)S(1)} %collective-permute-done.1.other, f32[1024,1152]{1,0:T(8,128)S(1)} %get-tuple-element.25.gq, ...), custom_call_target="tpu_custom_call" | custom-call | flops 3623878656 | bytes 3623878656 | tf_op jit(solution)/shard_map/pallas_call | solution.py:253
  37.9 0.0 collective-permute-done.other
  37.9 3.1 %shard_map.64 = (bf16[1024,1152]{1,0:T(8,128)(2,1)}, bf16[1024,1152]{1,0:T(8,128)(2,1)}) custom-call(f32[8,128]{1,0:T(8,128)S(1)} %get-tuple-element.21.consts, bf16[1024,1152]{1,0:T(8,128)(2,1)S(1)} %get-tuple-element.22.zq, bf16[256,1152]{1,0:T(8,128)(2,1)S(1)} %collective-permute-done.other, f32[1024,1152]{1,0:T(8,128)S(1)} %get-tuple-element.30.so_far, ...), custom_call_target="tpu_custom_call" | custom-call | flops 1207959552 | bytes 1207959552 | tf_op jit(solution)/shard_map/pallas_call | solution.py:257
Async XLA Ops:
  2.3 31.1 %collective-permute-start.1 = (bf16[768,1152]{1,0:T(8,128)(2,1)S(1)}, bf16[768,1152]{1,0:T(8,128)(2,1)S(1)}, u32[]{:S(2)}, u32[]{:S(2)}) collective-permute-start(bf16[768,1152]{1,0:T(8,128)(2,1)S(1)} %get-tuple-element.19.z1), channel_id=1, source_target_pairs={{0,255},{1,2},{2,1},{3,4},{4,3},{5,6},{6,5},{7,8},{8,7},{9,10},{10... | collective-permute-start | bytes 5308424 | tf_op jit(solution)/shard_map/ppermute | solution.py:231
  8.8 29.1 %collective-permute-start = (bf16[256,1152]{1,0:T(8,128)(2,1)S(1)}, bf16[256,1152]{1,0:T(8,128)(2,1)S(1)}, u32[]{:S(2)}, u32[]{:S(2)}) collective-permute-start(bf16[256,1152]{1,0:T(8,128)(2,1)S(1)} %get-tuple-element.23), channel_id=1, source_target_pairs={{0,255},{1,2},{2,1},{3,4},{4,3},{5,6},{6,5},{7,8},{8,7},{9,10},{10... | collective-permute-start | bytes 1769480 | tf_op jit(solution)/shard_map/ppermute | solution.py:243
  8.9 15.3 %collective-permute-start.2 = (bf16[1024,1152]{1,0:T(8,128)(2,1)S(1)}, bf16[1024,1152]{1,0:T(8,128)(2,1)S(1)}, u32[]{:S(2)}, u32[]{:S(2)}) collective-permute-start(bf16[1024,1152]{1,0:T(8,128)(2,1)S(1)} %get-tuple-element.24.zp), channel_id=1, source_target_pairs={{0,1},{1,0},{2,3},{3,2},{4,5},{5,4},{6,7},{7,6},{8,9},{9,8},{10,11... | collective-permute-start | bytes 7077896 | tf_op jit(solution)/shard_map/ppermute | solution.py:242

commit v5 on v3

--- a/solution.py
+++ b/solution.py
@@ -11,6 +11,7 @@
 LOG2_E = 1.4426950408889634
 F32, BF16 = jnp.float32, jnp.bfloat16
 BLOCK = 256
+HALF = BLOCK // 2
 FIRST = 768
 MIB = 2**20
 
@@ -145,15 +146,13 @@
     return raw2[there, :], inv2[there, :]
 
 
-def far_kernel(
-    consts, zq, other, gq, raw1, raw2, inv1, inv2, after_near, so_far
-):
+def far_kernel(consts, zq, other, gq, after_near, so_far):
     multiplier, scale, shift = constants(consts)
     for here in blocks(zq.shape[0]):
         power = exponential(rows_dot_rows(zq[here, :], other[...]), scale, shift)
         factors = (multiplier / (1.0 + power)).astype(BF16)
         total = gq[here, :] + dot(factors, other[...])
-        so_far[here, :] = backward(*raw_block(here, raw1, raw2, inv1, inv2), total)
+        so_far[here, :] = total
 
 
 def last_kernel(
@@ -169,16 +168,18 @@
         agreement = ahead
         if i + 1 < len(pieces):
             ahead = rows_dot_rows(zq[pieces[i + 1], :], other[...])
-        factors = multiplier / (1.0 + exponential(agreement, scale, shift))
-        inner = jnp.sum(factors * agreement, axis=-1, keepdims=True)
-        term = dot(factors.astype(BF16), other[...])
+        factors = (multiplier / (1.0 + exponential(agreement, scale, shift))).astype(BF16)
+        total = so_far[here, :] + dot(factors, other[...])
         raw, inverse = raw_block(here, raw1, raw2, inv1, inv2)
-        more = inverse * term - raw.astype(F32) * (inverse * inverse * inner)
-        held[here, :] = (so_far[here, :] + more).astype(BF16)
-        put(parity, image_out, text_out, here, held.at[here], sems.at[i])
+        for j in range(2):
+            half = slice(j * HALF, (j + 1) * HALF)
+            there = slice(here.start + half.start, here.start + half.stop)
+            held[there, :] = backward(raw[half, :], inverse[half, :], total[half, :]).astype(BF16)
+            put(parity, image_out, text_out, there, held.at[there], sems.at[2 * i + j])
     pltpu.make_async_copy(grad, image_out.at[everything], grad_sem).wait()
-    for i, here in enumerate(pieces):
-        pltpu.make_async_copy(held.at[here], image_out.at[here], sems.at[i]).wait()
+    for i in range(zq.shape[0] // HALF):
+        there = pl.ds(i * HALF, HALF)
+        pltpu.make_async_copy(held.at[there], image_out.at[there], sems.at[i]).wait()
 
 
 def shape(rows, columns, kind):
@@ -240,13 +241,13 @@
     )(consts, zp, zq, coef, near_block, rawp, invp)
     so_far = call(
         far_kernel, shape(rows, width, F32),
-        [VMEM] * 9, VMEM, [], 8, 2 * product * first // rows,
-    )(consts, zq, far1, gq, raw1, raw2, inv1, inv2, grad)
+        [VMEM] * 5, VMEM, [], 8, 2 * product * first // rows,
+    )(consts, zq, far1, gq, grad)
     return call(
         last_kernel,
         (pltpu.HBM((rows, width), BF16),) * 2,
         [VMEM] * 9, (HBM, HBM),
-        [pltpu.VMEM((rows, width), BF16), dma((rows // BLOCK,)), dma], 12, 2 * product * rest // rows,
+        [pltpu.VMEM((rows, width), BF16), dma((rows // HALF,)), dma], 12, 2 * product * rest // rows,
     )(consts, zq, far2, so_far, raw1, raw2, inv1, inv2, grad)
 
 

time: 41.7 us -> 41.4 us (level)
    pallas_call x1, Pallas kernels: 5.58 us -> 4.61 us  [on_device(): call(far_kernel, shape(rows, width, F32), [VMEM] * 5, VMEM, [], 8, 2 * pr...]
    pallas_call x1, Pallas kernels: 3.11 us -> 3.73 us  [on_device(): call(last_kernel, (pltpu.HBM((rows, width), BF16),) * 2, [VMEM] * 9, (HBM...]
  transfers between devices with their start and end apart: 3 -> 3, of which waited for: 0 -> 0; matrix products, arithmetic and copies ran while one was open for 0% -> 0% of each run, Pallas kernels for 55% -> 53%
where the time goes in v5:
time: 41.4 us; the launch traced here: 41.2 us
  Pallas kernels  27.1 us (65%)
  starting transfers between devices  11.9 us (29%)
  between operations  2.17 us (5%)
    pallas_call x1, Pallas kernels, on_device(): call(near_kernel, shape(rows, width, BF16), [VMEM] * 7, VMEM, [], 12, 3 *...  9.13 us
    ppermute x1, starting transfers between devices, on_device(): near_block = lax.ppermute(zp, 'dp', near)  9.11 us
    pallas_call x1, Pallas kernels, on_device(): call(local_kernel, (shape(rows, rows, BF16), shape(rows, width, F32)), [V...  5.79 us
    pallas_call x1, Pallas kernels, on_device(): call(far_kernel, shape(rows, width, F32), [VMEM] * 5, VMEM, [], 8, 2 * pr...  4.61 us
    pallas_call x1, Pallas kernels, on_device(): call(last_kernel, (pltpu.HBM((rows, width), BF16),) * 2, [VMEM] * 9, (HBM...  3.73 us
    ppermute x1, starting transfers between devices, on_device(): far1 = lax.ppermute(z1, 'dp', far)  2.69 us
    pallas_call x1, Pallas kernels, on_device(): call(rest_kernel, (shape(rows, width, BF16), shape(rest, width, BF16), sh...  2.15 us
    pallas_call x1, Pallas kernels, on_device(): call(first_kernel, (shape(first, width, BF16), shape(first, width, BF16),...  1.71 us
  transfers between devices with their start and end apart: 3, of which 0 were waited for; matrix products, arithmetic and copies ran while one was open for 0% of the time, Pallas kernels for 53%

profile of v5, /device:TPU:1, one launch (start us, length us, event | category | flops | bytes accessed | tf_op | source)
XLA Modules:
  0.0 41.2 jit_solution(7073278642854081339)
XLA Ops:
  0.6 1.7 %shard_map.59 = (bf16[768,1152]{1,0:T(8,128)(2,1)S(1)}, bf16[768,1152]{1,0:T(8,128)(2,1)S(1)}, f32[768,1]{1,0:T(8,128)S(1)}) custom-call(bf16[1024,1152]{1,0:T(8,128)(2,1)} %image.3, bf16[1024,1152]{1,0:T(8,128)(2,1)} %text.3), custom_call_target="tpu_custom_call" | custom-call | flops 4831838208 | bytes 301989888 | tf_op jit(solution)/shard_map/pallas_call | solution.py:215
  2.3 2.7 %collective-permute-start.1 = (bf16[768,1152]{1,0:T(8,128)(2,1)S(1)}, bf16[768,1152]{1,0:T(8,128)(2,1)S(1)}, u32[]{:S(2)}, u32[]{:S(2)}) collective-permute-start(bf16[768,1152]{1,0:T(8,128)(2,1)S(1)} %get-tuple-element.15.z1), channel_id=1, source_target_pairs={{0,255},{1,2},{2,1},{3,4},{4,3},{5,6},{6,5},{7,8},{8,7},{9,10},{10... | collective-permute-start | bytes 5308424 | tf_op jit(solution)/shard_map/ppermute | solution.py:220
  6.3 2.1 %shard_map.60 = (bf16[1024,1152]{1,0:T(8,128)(2,1)S(1)}, bf16[256,1152]{1,0:T(8,128)(2,1)S(1)}, bf16[1024,1152]{1,0:T(8,128)(2,1)S(1)}, bf16[1024,1152]{1,0:T(8,...) custom-call(bf16[1024,1152]{1,0:T(8,128)(2,1)} %image.3, ...), custom_call_target="tpu_custom_call" | custom-call | flops 9663676416 | bytes 603979776 | tf_op jit(solution)/shard_map/pallas_call | solution.py:221
  8.5 0.1 collective-permute-start
  8.6 9.1 %collective-permute-start.2 = (bf16[1024,1152]{1,0:T(8,128)(2,1)S(1)}, bf16[1024,1152]{1,0:T(8,128)(2,1)S(1)}, u32[]{:S(2)}, u32[]{:S(2)}) collective-permute-start(bf16[1024,1152]{1,0:T(8,128)(2,1)S(1)} %get-tuple-element.19.zp), channel_id=1, source_target_pairs={{0,1},{1,0},{2,3},{3,2},{4,5},{5,4},{6,7},{7,6},{8,9},{9,8},{10,11... | collective-permute-start | bytes 7077896 | tf_op jit(solution)/shard_map/ppermute | solution.py:231
  17.7 5.8 %shard_map.61 = (bf16[1024,1024]{1,0:T(8,128)(2,1)S(1)}, f32[1024,1152]{1,0:T(8,128)S(1)}) custom-call(f32[8,128]{1,0:T(8,128)S(1)} %get-tuple-element.16.consts, bf16[1024,1152]{1,0:T(8,128)(2,1)S(1)} %get-tuple-element.19.zp, bf16[1024,1152]{1,0:T(8,128)(2,1)S(1)} %get-tuple-element.17.zq), custom_call_target="tpu_custom_call" | custom-call | flops 77309411328 | bytes 4831838208 | tf_op jit(solution)/shard_map/pallas_call | solution.py:233
  23.5 0.0 collective-permute-done.2.other
  23.5 9.1 %shard_map.62.after_near.grad = bf16[1024,1152]{1,0:T(8,128)(2,1)S(1)} custom-call(f32[8,128]{1,0:T(8,128)S(1)} %get-tuple-element.16.consts, bf16[1024,1152]{1,0:T(8,128)(2,1)S(1)} %get-tuple-element.19.zp, bf16[1024,1152]{1,0:T(8,128)(2,1)S(1)} %get-tuple-element.17.zq, bf16[1024,1024]{1,0:T(8,128)(2,1)S(1)} %get-tuple-element.21.coef, ...), custom_call_target="tpu_custom_call" | custom-call | flops 7247757312 | bytes 7247757312 | tf_op jit(solution)/shard_map/pallas_call | solution.py:238
  32.6 0.0 collective-permute-done.1.other
  32.7 4.6 %shard_map.63.so_far = f32[1024,1152]{1,0:T(8,128)S(1)} custom-call(f32[8,128]{1,0:T(8,128)S(1)} %get-tuple-element.16.consts, bf16[1024,1152]{1,0:T(8,128)(2,1)S(1)} %get-tuple-element.17.zq, bf16[768,1152]{1,0:T(8,128)(2,1)S(1)} %collective-permute-done.1.other, f32[1024,1152]{1,0:T(8,128)S(1)} %get-tuple-element.20.gq, ...), custom_call_target="tpu_custom_call" | custom-call | flops 3623878656 | bytes 3623878656 | tf_op jit(solution)/shard_map/pallas_call | solution.py:242
  37.3 0.0 collective-permute-done.other
  37.3 3.7 %shard_map.64 = (bf16[1024,1152]{1,0:T(8,128)(2,1)}, bf16[1024,1152]{1,0:T(8,128)(2,1)}) custom-call(f32[8,128]{1,0:T(8,128)S(1)} %get-tuple-element.16.consts, bf16[1024,1152]{1,0:T(8,128)(2,1)S(1)} %get-tuple-element.17.zq, bf16[256,1152]{1,0:T(8,128)(2,1)S(1)} %collective-permute-done.other, f32[1024,1152]{1,0:T(8,128)S(1)} %shard_map.63.so_far, ...), custom_call_target="tpu_custom_call" | custom-call | flops 1207959552 | bytes 1207959552 | tf_op jit(solution)/shard_map/pallas_call | solution.py:246
Async XLA Ops:
  2.3 30.3 %collective-permute-start.1 = (bf16[768,1152]{1,0:T(8,128)(2,1)S(1)}, bf16[768,1152]{1,0:T(8,128)(2,1)S(1)}, u32[]{:S(2)}, u32[]{:S(2)}) collective-permute-start(bf16[768,1152]{1,0:T(8,128)(2,1)S(1)} %get-tuple-element.15.z1), channel_id=1, source_target_pairs={{0,255},{1,2},{2,1},{3,4},{4,3},{5,6},{6,5},{7,8},{8,7},{9,10},{10... | collective-permute-start | bytes 5308424 | tf_op jit(solution)/shard_map/ppermute | solution.py:220
  8.5 28.8 %collective-permute-start = (bf16[256,1152]{1,0:T(8,128)(2,1)S(1)}, bf16[256,1152]{1,0:T(8,128)(2,1)S(1)}, u32[]{:S(2)}, u32[]{:S(2)}) collective-permute-start(bf16[256,1152]{1,0:T(8,128)(2,1)S(1)} %get-tuple-element.18), channel_id=1, source_target_pairs={{0,255},{1,2},{2,1},{3,4},{4,3},{5,6},{6,5},{7,8},{8,7},{9,10},{10... | collective-permute-start | bytes 1769480 | tf_op jit(solution)/shard_map/ppermute | solution.py:232
  8.6 14.9 %collective-permute-start.2 = (bf16[1024,1152]{1,0:T(8,128)(2,1)S(1)}, bf16[1024,1152]{1,0:T(8,128)(2,1)S(1)}, u32[]{:S(2)}, u32[]{:S(2)}) collective-permute-start(bf16[1024,1152]{1,0:T(8,128)(2,1)S(1)} %get-tuple-element.19.zp), channel_id=1, source_target_pairs={{0,1},{1,0},{2,3},{3,2},{4,5},{5,4},{6,7},{7,6},{8,9},{9,8},{10,11... | collective-permute-start | bytes 7077896 | tf_op jit(solution)/shard_map/ppermute | solution.py:231

commit v6 on v4

--- a/solution.py
+++ b/solution.py
@@ -11,6 +11,7 @@
 LOG2_E = 1.4426950408889634
 F32, BF16 = jnp.float32, jnp.bfloat16
 BLOCK = 256
+HALF = BLOCK // 2
 FIRST = 768
 MIB = 2**20
 
@@ -165,9 +166,9 @@
         agreement = ahead
         if i + 1 < len(pieces):
             ahead = rows_dot_rows(zq[pieces[i + 1], :], other[...])
-        factors = multiplier / (1.0 + exponential(agreement, scale, shift))
-        along = jnp.sum(factors * agreement, axis=-1, keepdims=True)
-        yield i, here, dot(factors.astype(BF16), other[...]), along
+        factors = (multiplier / (1.0 + exponential(agreement, scale, shift))).astype(BF16)
+        along = jnp.sum(factors.astype(F32) * agreement, axis=-1, keepdims=True)
+        yield i, here, dot(factors, other[...]), along
 
 
 def far_kernel(consts, zq, other, gq, along_in, after_near, so_far, along_out):
@@ -186,11 +187,15 @@
         raw, inverse = raw_block(here, raw1, raw2, inv1, inv2)
         inner = ratio[here, :] * (along_in[here, :] + along)
         total = so_far[here, :] + term
-        held[here, :] = (inverse * total - raw.astype(F32) * (inverse * inverse * inner)).astype(BF16)
-        put(parity, image_out, text_out, here, held.at[here], sems.at[i])
+        back = (inverse * total - raw.astype(F32) * (inverse * inverse * inner)).astype(BF16)
+        for j in range(2):
+            there = slice(here.start + j * HALF, here.start + (j + 1) * HALF)
+            held[there, :] = back[j * HALF : (j + 1) * HALF, :]
+            put(parity, image_out, text_out, there, held.at[there], sems.at[2 * i + j])
     pltpu.make_async_copy(grad, image_out.at[everything], grad_sem).wait()
-    for i, here in enumerate(blocks(zq.shape[0])):
-        pltpu.make_async_copy(held.at[here], image_out.at[here], sems.at[i]).wait()
+    for i in range(zq.shape[0] // HALF):
+        there = pl.ds(i * HALF, HALF)
+        pltpu.make_async_copy(held.at[there], image_out.at[there], sems.at[i]).wait()
 
 
 def shape(rows, columns, kind):
@@ -258,7 +263,7 @@
         last_kernel,
         (pltpu.HBM((rows, width), BF16),) * 2,
         [VMEM] * 11, (HBM, HBM),
-        [pltpu.VMEM((rows, width), BF16), dma((rows // BLOCK,)), dma], 12, 2 * product * rest // rows,
+        [pltpu.VMEM((rows, width), BF16), dma((rows // HALF,)), dma], 12, 2 * product * rest // rows,
     )(consts, zq, far2, so_far, along, ratio, raw1, raw2, inv1, inv2, grad)
 
 

time: 41.3 us -> 41.5 us (level)
  no operation moved by 1% of the time
where the time goes in v6:
time: 41.5 us; the launch traced here: 41.3 us
  Pallas kernels  27.3 us (66%)
  starting transfers between devices  11.9 us (29%)
  between operations  2.16 us (5%)
    pallas_call x1, Pallas kernels, on_device(): call(near_kernel, shape(rows, width, BF16), [VMEM] * 7, VMEM, [], 12, 3 *...  9.2 us
    ppermute x1, starting transfers between devices, on_device(): near_block = lax.ppermute(zp, 'dp', near)  9.11 us
    pallas_call x1, Pallas kernels, on_device(): call(local_kernel, (shape(rows, rows, BF16), shape(rows, width, F32), sha...  6.17 us
    pallas_call x1, Pallas kernels, on_device(): call(far_kernel, (shape(rows, width, F32), shape(rows, 1, F32)), [VMEM] *...  4.48 us
    pallas_call x1, Pallas kernels, on_device(): call(last_kernel, (pltpu.HBM((rows, width), BF16),) * 2, [VMEM] * 11, (HB...  3.24 us
    ppermute x1, starting transfers between devices, on_device(): far1 = lax.ppermute(z1, 'dp', far)  2.69 us
    pallas_call x1, Pallas kernels, on_device(): call(rest_kernel, (shape(rows, width, BF16), shape(rest, width, BF16), sh...  2.46 us
    pallas_call x1, Pallas kernels, on_device(): call(first_kernel, (shape(first, width, BF16), shape(first, width, BF16),...  1.71 us
  transfers between devices with their start and end apart: 3, of which 0 were waited for; matrix products, arithmetic and copies ran while one was open for 0% of the time, Pallas kernels for 54%

profile of v6, /device:TPU:1, one launch (start us, length us, event | category | flops | bytes accessed | tf_op | source)
XLA Modules:
  0.0 41.3 jit_solution(1654583474158741075)
XLA Ops:
  0.6 1.7 %shard_map.59 = (bf16[768,1152]{1,0:T(8,128)(2,1)S(1)}, bf16[768,1152]{1,0:T(8,128)(2,1)S(1)}, f32[768,1]{1,0:T(8,128)S(1)}) custom-call(bf16[1024,1152]{1,0:T(8,128)(2,1)} %image.3, bf16[1024,1152]{1,0:T(8,128)(2,1)} %text.3), custom_call_target="tpu_custom_call" | custom-call | flops 4831838208 | bytes 301989888 | tf_op jit(solution)/shard_map/pallas_call | solution.py:231
  2.3 2.7 %collective-permute-start.1 = (bf16[768,1152]{1,0:T(8,128)(2,1)S(1)}, bf16[768,1152]{1,0:T(8,128)(2,1)S(1)}, u32[]{:S(2)}, u32[]{:S(2)}) collective-permute-start(bf16[768,1152]{1,0:T(8,128)(2,1)S(1)} %get-tuple-element.19.z1), channel_id=1, source_target_pairs={{0,255},{1,2},{2,1},{3,4},{4,3},{5,6},{6,5},{7,8},{8,7},{9,10},{10... | collective-permute-start | bytes 5308424 | tf_op jit(solution)/shard_map/ppermute | solution.py:236
  6.3 2.5 %shard_map.60 = (bf16[1024,1152]{1,0:T(8,128)(2,1)S(1)}, bf16[256,1152]{1,0:T(8,128)(2,1)S(1)}, bf16[1024,1152]{1,0:T(8,128)(2,1)S(1)}, bf16[1024,1152]{1,0:T(8,...) custom-call(bf16[1024,1152]{1,0:T(8,128)(2,1)} %image.3, ...), custom_call_target="tpu_custom_call" | custom-call | flops 9663676416 | bytes 603979776 | tf_op jit(solution)/shard_map/pallas_call | solution.py:237
  8.8 0.1 collective-permute-start
  8.9 9.1 %collective-permute-start.2 = (bf16[1024,1152]{1,0:T(8,128)(2,1)S(1)}, bf16[1024,1152]{1,0:T(8,128)(2,1)S(1)}, u32[]{:S(2)}, u32[]{:S(2)}) collective-permute-start(bf16[1024,1152]{1,0:T(8,128)(2,1)S(1)} %get-tuple-element.24.zp), channel_id=1, source_target_pairs={{0,1},{1,0},{2,3},{3,2},{4,5},{5,4},{6,7},{7,6},{8,9},{9,8},{10,11... | collective-permute-start | bytes 7077896 | tf_op jit(solution)/shard_map/ppermute | solution.py:247
  18.0 6.2 %shard_map.61 = (bf16[1024,1024]{1,0:T(8,128)(2,1)S(1)}, f32[1024,1152]{1,0:T(8,128)S(1)}, f32[1024,1]{1,0:T(8,128)S(1)}) custom-call(f32[8,128]{1,0:T(8,128)S(1)} %get-tuple-element.21.consts, bf16[1024,1152]{1,0:T(8,128)(2,1)S(1)} %get-tuple-element.24.zp, bf16[1024,1152]{1,0:T(8,128)(2,1)S(1)} %get-tuple-element.22.zq), custom_call_target="tpu_custom_call" | custom-call | flops 77309411328 | bytes 4831838208 | tf_op jit(solution)/shard_map/pallas_call | solution.py:249
  24.2 0.0 collective-permute-done.2.other
  24.2 9.2 %shard_map.62.after_near.grad = bf16[1024,1152]{1,0:T(8,128)(2,1)S(1)} custom-call(f32[8,128]{1,0:T(8,128)S(1)} %get-tuple-element.21.consts, bf16[1024,1152]{1,0:T(8,128)(2,1)S(1)} %get-tuple-element.24.zp, bf16[1024,1152]{1,0:T(8,128)(2,1)S(1)} %get-tuple-element.22.zq, bf16[1024,1024]{1,0:T(8,128)(2,1)S(1)} %get-tuple-element.27.coef, ...), custom_call_target="tpu_custom_call" | custom-call | flops 7247757312 | bytes 7247757312 | tf_op jit(solution)/shard_map/pallas_call | solution.py:254
  33.4 0.0 collective-permute-done.1.other
  33.4 4.5 %shard_map.63 = (f32[1024,1152]{1,0:T(8,128)S(1)}, f32[1024,1]{1,0:T(8,128)S(1)}) custom-call(f32[8,128]{1,0:T(8,128)S(1)} %get-tuple-element.21.consts, bf16[1024,1152]{1,0:T(8,128)(2,1)S(1)} %get-tuple-element.22.zq, bf16[768,1152]{1,0:T(8,128)(2,1)S(1)} %collective-permute-done.1.other, f32[1024,1152]{1,0:T(8,128)S(1)} %get-tuple-element.25.gq, ...), custom_call_target="tpu_custom_call" | custom-call | flops 3623878656 | bytes 3623878656 | tf_op jit(solution)/shard_map/pallas_call | solution.py:258
  37.9 0.0 collective-permute-done.other
  37.9 3.2 %shard_map.64 = (bf16[1024,1152]{1,0:T(8,128)(2,1)}, bf16[1024,1152]{1,0:T(8,128)(2,1)}) custom-call(f32[8,128]{1,0:T(8,128)S(1)} %get-tuple-element.21.consts, bf16[1024,1152]{1,0:T(8,128)(2,1)S(1)} %get-tuple-element.22.zq, bf16[256,1152]{1,0:T(8,128)(2,1)S(1)} %collective-permute-done.other, f32[1024,1152]{1,0:T(8,128)S(1)} %get-tuple-element.30.so_far, ...), custom_call_target="tpu_custom_call" | custom-call | flops 1207959552 | bytes 1207959552 | tf_op jit(solution)/shard_map/pallas_call | solution.py:262
Async XLA Ops:
  2.3 31.1 %collective-permute-start.1 = (bf16[768,1152]{1,0:T(8,128)(2,1)S(1)}, bf16[768,1152]{1,0:T(8,128)(2,1)S(1)}, u32[]{:S(2)}, u32[]{:S(2)}) collective-permute-start(bf16[768,1152]{1,0:T(8,128)(2,1)S(1)} %get-tuple-element.19.z1), channel_id=1, source_target_pairs={{0,255},{1,2},{2,1},{3,4},{4,3},{5,6},{6,5},{7,8},{8,7},{9,10},{10... | collective-permute-start | bytes 5308424 | tf_op jit(solution)/shard_map/ppermute | solution.py:236
  8.8 29.1 %collective-permute-start = (bf16[256,1152]{1,0:T(8,128)(2,1)S(1)}, bf16[256,1152]{1,0:T(8,128)(2,1)S(1)}, u32[]{:S(2)}, u32[]{:S(2)}) collective-permute-start(bf16[256,1152]{1,0:T(8,128)(2,1)S(1)} %get-tuple-element.23), channel_id=1, source_target_pairs={{0,255},{1,2},{2,1},{3,4},{4,3},{5,6},{6,5},{7,8},{8,7},{9,10},{10... | collective-permute-start | bytes 1769480 | tf_op jit(solution)/shard_map/ppermute | solution.py:248
  8.9 15.3 %collective-permute-start.2 = (bf16[1024,1152]{1,0:T(8,128)(2,1)S(1)}, bf16[1024,1152]{1,0:T(8,128)(2,1)S(1)}, u32[]{:S(2)}, u32[]{:S(2)}) collective-permute-start(bf16[1024,1152]{1,0:T(8,128)(2,1)S(1)} %get-tuple-element.24.zp), channel_id=1, source_target_pairs={{0,1},{1,0},{2,3},{3,2},{4,5},{5,4},{6,7},{7,6},{8,9},{9,8},{10,11... | collective-permute-start | bytes 7077896 | tf_op jit(solution)/shard_map/ppermute | solution.py:247

commit v7 on v5

--- a/solution.py
+++ b/solution.py
@@ -148,11 +148,14 @@
 
 def far_kernel(consts, zq, other, gq, after_near, so_far):
     multiplier, scale, shift = constants(consts)
-    for here in blocks(zq.shape[0]):
-        power = exponential(rows_dot_rows(zq[here, :], other[...]), scale, shift)
-        factors = (multiplier / (1.0 + power)).astype(BF16)
-        total = gq[here, :] + dot(factors, other[...])
-        so_far[here, :] = total
+    pieces = blocks(zq.shape[0])
+    ahead = rows_dot_rows(zq[pieces[0], :], other[...])
+    for i, here in enumerate(pieces):
+        agreement = ahead
+        if i + 1 < len(pieces):
+            ahead = rows_dot_rows(zq[pieces[i + 1], :], other[...])
+        factors = (multiplier / (1.0 + exponential(agreement, scale, shift))).astype(BF16)
+        so_far[here, :] = gq[here, :] + dot(factors, other[...])
 
 
 def last_kernel(

time: 41.4 us -> 41.2 us (level)
  transfers between devices with their start and end apart: 3 -> 3, of which waited for: 0 -> 0; matrix products, arithmetic and copies ran while one was open for 0% -> 0% of each run, Pallas kernels for 53% -> 52%
where the time goes in v7:
time: 41.2 us; the launch traced here: 40.9 us
  Pallas kernels  26.9 us (65%)
  starting transfers between devices  11.9 us (29%)
  between operations  2.17 us (5%)
    pallas_call x1, Pallas kernels, on_device(): call(near_kernel, shape(rows, width, BF16), [VMEM] * 7, VMEM, [], 12, 3 *...  9.13 us
    ppermute x1, starting transfers between devices, on_device(): near_block = lax.ppermute(zp, 'dp', near)  9.11 us
    pallas_call x1, Pallas kernels, on_device(): call(local_kernel, (shape(rows, rows, BF16), shape(rows, width, F32)), [V...  5.79 us
    pallas_call x1, Pallas kernels, on_device(): call(far_kernel, shape(rows, width, F32), [VMEM] * 5, VMEM, [], 8, 2 * pr...  4.36 us
    pallas_call x1, Pallas kernels, on_device(): call(last_kernel, (pltpu.HBM((rows, width), BF16),) * 2, [VMEM] * 9, (HBM...  3.73 us
    ppermute x1, starting transfers between devices, on_device(): far1 = lax.ppermute(z1, 'dp', far)  2.69 us
    pallas_call x1, Pallas kernels, on_device(): call(rest_kernel, (shape(rows, width, BF16), shape(rest, width, BF16), sh...  2.15 us
    pallas_call x1, Pallas kernels, on_device(): call(first_kernel, (shape(first, width, BF16), shape(first, width, BF16),...  1.71 us
  transfers between devices with their start and end apart: 3, of which 0 were waited for; matrix products, arithmetic and copies ran while one was open for 0% of the time, Pallas kernels for 52%

profile of v7, /device:TPU:1, one launch (start us, length us, event | category | flops | bytes accessed | tf_op | source)
XLA Modules:
  0.0 40.9 jit_solution(2902017724614387452)
XLA Ops:
  0.6 1.7 %shard_map.59 = (bf16[768,1152]{1,0:T(8,128)(2,1)S(1)}, bf16[768,1152]{1,0:T(8,128)(2,1)S(1)}, f32[768,1]{1,0:T(8,128)S(1)}) custom-call(bf16[1024,1152]{1,0:T(8,128)(2,1)} %image.3, bf16[1024,1152]{1,0:T(8,128)(2,1)} %text.3), custom_call_target="tpu_custom_call" | custom-call | flops 4831838208 | bytes 301989888 | tf_op jit(solution)/shard_map/pallas_call | solution.py:218
  2.3 2.7 %collective-permute-start.1 = (bf16[768,1152]{1,0:T(8,128)(2,1)S(1)}, bf16[768,1152]{1,0:T(8,128)(2,1)S(1)}, u32[]{:S(2)}, u32[]{:S(2)}) collective-permute-start(bf16[768,1152]{1,0:T(8,128)(2,1)S(1)} %get-tuple-element.15.z1), channel_id=1, source_target_pairs={{0,255},{1,2},{2,1},{3,4},{4,3},{5,6},{6,5},{7,8},{8,7},{9,10},{10... | collective-permute-start | bytes 5308424 | tf_op jit(solution)/shard_map/ppermute | solution.py:223
  6.3 2.1 %shard_map.60 = (bf16[1024,1152]{1,0:T(8,128)(2,1)S(1)}, bf16[256,1152]{1,0:T(8,128)(2,1)S(1)}, bf16[1024,1152]{1,0:T(8,128)(2,1)S(1)}, bf16[1024,1152]{1,0:T(8,...) custom-call(bf16[1024,1152]{1,0:T(8,128)(2,1)} %image.3, ...), custom_call_target="tpu_custom_call" | custom-call | flops 9663676416 | bytes 603979776 | tf_op jit(solution)/shard_map/pallas_call | solution.py:224
  8.5 0.1 collective-permute-start
  8.6 9.1 %collective-permute-start.2 = (bf16[1024,1152]{1,0:T(8,128)(2,1)S(1)}, bf16[1024,1152]{1,0:T(8,128)(2,1)S(1)}, u32[]{:S(2)}, u32[]{:S(2)}) collective-permute-start(bf16[1024,1152]{1,0:T(8,128)(2,1)S(1)} %get-tuple-element.19.zp), channel_id=1, source_target_pairs={{0,1},{1,0},{2,3},{3,2},{4,5},{5,4},{6,7},{7,6},{8,9},{9,8},{10,11... | collective-permute-start | bytes 7077896 | tf_op jit(solution)/shard_map/ppermute | solution.py:234
  17.7 5.8 %shard_map.61 = (bf16[1024,1024]{1,0:T(8,128)(2,1)S(1)}, f32[1024,1152]{1,0:T(8,128)S(1)}) custom-call(f32[8,128]{1,0:T(8,128)S(1)} %get-tuple-element.16.consts, bf16[1024,1152]{1,0:T(8,128)(2,1)S(1)} %get-tuple-element.19.zp, bf16[1024,1152]{1,0:T(8,128)(2,1)S(1)} %get-tuple-element.17.zq), custom_call_target="tpu_custom_call" | custom-call | flops 77309411328 | bytes 4831838208 | tf_op jit(solution)/shard_map/pallas_call | solution.py:236
  23.5 0.0 collective-permute-done.2.other
  23.5 9.1 %shard_map.62.after_near.grad = bf16[1024,1152]{1,0:T(8,128)(2,1)S(1)} custom-call(f32[8,128]{1,0:T(8,128)S(1)} %get-tuple-element.16.consts, bf16[1024,1152]{1,0:T(8,128)(2,1)S(1)} %get-tuple-element.19.zp, bf16[1024,1152]{1,0:T(8,128)(2,1)S(1)} %get-tuple-element.17.zq, bf16[1024,1024]{1,0:T(8,128)(2,1)S(1)} %get-tuple-element.21.coef, ...), custom_call_target="tpu_custom_call" | custom-call | flops 7247757312 | bytes 7247757312 | tf_op jit(solution)/shard_map/pallas_call | solution.py:241
  32.6 0.0 collective-permute-done.1.other
  32.7 4.4 %shard_map.63.so_far = f32[1024,1152]{1,0:T(8,128)S(1)} custom-call(f32[8,128]{1,0:T(8,128)S(1)} %get-tuple-element.16.consts, bf16[1024,1152]{1,0:T(8,128)(2,1)S(1)} %get-tuple-element.17.zq, bf16[768,1152]{1,0:T(8,128)(2,1)S(1)} %collective-permute-done.1.other, f32[1024,1152]{1,0:T(8,128)S(1)} %get-tuple-element.20.gq, ...), custom_call_target="tpu_custom_call" | custom-call | flops 3623878656 | bytes 3623878656 | tf_op jit(solution)/shard_map/pallas_call | solution.py:245
  37.0 0.0 collective-permute-done.other
  37.0 3.7 %shard_map.64 = (bf16[1024,1152]{1,0:T(8,128)(2,1)}, bf16[1024,1152]{1,0:T(8,128)(2,1)}) custom-call(f32[8,128]{1,0:T(8,128)S(1)} %get-tuple-element.16.consts, bf16[1024,1152]{1,0:T(8,128)(2,1)S(1)} %get-tuple-element.17.zq, bf16[256,1152]{1,0:T(8,128)(2,1)S(1)} %collective-permute-done.other, f32[1024,1152]{1,0:T(8,128)S(1)} %shard_map.63.so_far, ...), custom_call_target="tpu_custom_call" | custom-call | flops 1207959552 | bytes 1207959552 | tf_op jit(solution)/shard_map/pallas_call | solution.py:249
Async XLA Ops:
  2.3 30.3 %collective-permute-start.1 = (bf16[768,1152]{1,0:T(8,128)(2,1)S(1)}, bf16[768,1152]{1,0:T(8,128)(2,1)S(1)}, u32[]{:S(2)}, u32[]{:S(2)}) collective-permute-start(bf16[768,1152]{1,0:T(8,128)(2,1)S(1)} %get-tuple-element.15.z1), channel_id=1, source_target_pairs={{0,255},{1,2},{2,1},{3,4},{4,3},{5,6},{6,5},{7,8},{8,7},{9,10},{10... | collective-permute-start | bytes 5308424 | tf_op jit(solution)/shard_map/ppermute | solution.py:223
  8.5 28.5 %collective-permute-start = (bf16[256,1152]{1,0:T(8,128)(2,1)S(1)}, bf16[256,1152]{1,0:T(8,128)(2,1)S(1)}, u32[]{:S(2)}, u32[]{:S(2)}) collective-permute-start(bf16[256,1152]{1,0:T(8,128)(2,1)S(1)} %get-tuple-element.18), channel_id=1, source_target_pairs={{0,255},{1,2},{2,1},{3,4},{4,3},{5,6},{6,5},{7,8},{8,7},{9,10},{10... | collective-permute-start | bytes 1769480 | tf_op jit(solution)/shard_map/ppermute | solution.py:235
  8.6 14.9 %collective-permute-start.2 = (bf16[1024,1152]{1,0:T(8,128)(2,1)S(1)}, bf16[1024,1152]{1,0:T(8,128)(2,1)S(1)}, u32[]{:S(2)}, u32[]{:S(2)}) collective-permute-start(bf16[1024,1152]{1,0:T(8,128)(2,1)S(1)} %get-tuple-element.19.zp), channel_id=1, source_target_pairs={{0,1},{1,0},{2,3},{3,2},{4,5},{5,4},{6,7},{7,6},{8,9},{9,8},{10,11... | collective-permute-start | bytes 7077896 | tf_op jit(solution)/shard_map/ppermute | solution.py:234
